TPU v7x, 256 devices: a whole 4x4x8 slice. The times are simulated.
256 devices in a mesh: front: 32 (over z, x), row: 4 (over y), col: 2 (over core).
Axes of the slice: x: 4, y: 4, z: 8, core: 2. Of those that a mesh axis runs over, the one named last changes fastest.
Arguments:
- panel: float32 [32, 32, 512, 512], P('front', None, 'row', 'col'), may hold values from -6 to 13
- children: float32 [64, 4, 512, 512], P('front', None, 'row', 'col'), may hold values from -3 to 3
- parents: int32 [64], replicated, may hold values from 0 to 31, as said below
- row_maps: int32 [64, 16], replicated, may hold values from 0 to 127, as said below
- orders: int32 [32], P('front'), may hold values from 8192 to 16384, as said below
- pivots: int32 [32], P('front'), may hold values from 1 to 256, as said below
Outputs:
- factored: float32 [32, 32, 512, 512], P('front', None, 'row', 'col')
Inputs may be any that keep to these rules, and one draw needn't show every extreme that they name: `parents`: child 2 * d has parent p(d) and child 2 * d + 1 has parent (p(d) + r) mod 32, where p is a permutation of the fronts and r is one number in 1 to 31. The row blocks of one child map to distinct blocks, all below orders[parents[c]] / 128; row_maps[c, i] - i is a multiple of 4. Some child reaches block 127. `orders`: multiples of 128; some front has order 16384. Some front has 256 pivots.
All inputs are finite; a program needn't handle non-finite values.
Results may differ from a plain program's by a relative error of at most 0.0003.
Values sent between devices are 32-bit elements; how exact they have to be, the bound alone decides.
No kernel may reach another device: no remote copies, remote signals or barrier semaphores. Data moves between devices by JAX's collectives and lax.ppermute only.
A program may use at most 192 MiB of HBM per device.

v0:
```python
import jax
import jax.numpy as jnp
from jax import lax
from jax.sharding import PartitionSpec as P


def broadcast(value, axis, root):
    mine = lax.axis_index(axis) == root
    return lax.psum(jnp.where(mine, value, jnp.zeros_like(value)), axis)


def row_pick(matrix, first_block, row_index, rows_axis, blocks):
    picked = []
    for within in range(blocks):
        block_id = first_block + within
        cycle_at = block_id // rows_axis
        owner = block_id % rows_axis == row_index
        chosen = lax.dynamic_index_in_dim(matrix, cycle_at, 0, keepdims=False)
        picked.append(jnp.where(owner, chosen, jnp.zeros_like(chosen)))
    return jnp.concatenate(picked, 0)


def factor_panel(source, diag_rows, active, row_glob, panel_at, row_index, rows_axis, blocks):
    block_rows = source.shape[1]
    width = source.shape[2]
    first_col = panel_at * width
    mirrored = jnp.tril(diag_rows) + jnp.tril(diag_rows, -1).T
    masked = mirrored * active[:, None] * active[None, :] + jnp.diag(1.0 - active)
    factor = jnp.linalg.cholesky(masked)
    filled = source
    for within in range(blocks):
        block_id = panel_at * blocks + within
        cycle_at = block_id // rows_axis
        owner = block_id % rows_axis == row_index
        filled = filled.at[cycle_at].set(
            jnp.where(
                owner, mirrored[within * block_rows : (within + 1) * block_rows], filled[cycle_at]
            )
        )
    flat_rows = (filled * active[None, None, :]).reshape(-1, width)
    solved = lax.linalg.triangular_solve(
        factor, flat_rows, left_side=False, lower=True, transpose_a=True
    )
    solved = solved.reshape(source.shape)
    return jnp.where(row_glob >= first_col, solved, jnp.zeros_like(solved))


def on_device(panel, children, parents, row_maps, orders, pivots):
    rows_axis = lax.axis_size("row")
    front_index = lax.axis_index("front")
    row_index = lax.axis_index("row")
    col_index = lax.axis_index("col")
    cycles = panel.shape[1]
    block_rows = panel.shape[2]
    width = panel.shape[3]
    child_cycles = children.shape[1]
    current = panel[0]
    pieces = lax.all_gather(children, "front", axis=0, tiled=True)
    count_rows = pieces.shape[0]
    owned_mask = (parents == front_index).astype(jnp.float32)
    child_maps = row_maps
    child_maps = child_maps.reshape(count_rows, child_cycles, rows_axis)
    target = lax.dynamic_index_in_dim(child_maps, row_index, 2, keepdims=False) // rows_axis
    current = current.at[target].add(pieces * owned_mask[:, None, None, None])
    cycle_index_list = jnp.arange(cycles, dtype=jnp.int32)[:, None]
    local_rows = jnp.arange(block_rows, dtype=jnp.int32)[None, :]
    row_glob = ((cycle_index_list * rows_axis + row_index) * block_rows + local_rows)[:, :, None]
    col_glob = (col_index * width + jnp.arange(width, dtype=jnp.int32))[None, None, :]
    keep_mask = (row_glob >= col_glob) & (row_glob < orders[0])
    current = jnp.where(keep_mask, current, jnp.zeros_like(current))
    pivot_count = pivots[0]
    blocks = width // block_rows
    active = (0 + jnp.arange(width, dtype=jnp.int32) < pivot_count).astype(jnp.float32)
    diag_rows = lax.psum(row_pick(current, 0 * blocks, row_index, rows_axis, blocks), "row")
    panel_l = factor_panel(current, diag_rows, active, row_glob, 0, row_index, rows_axis, blocks)
    panel_l = broadcast(panel_l, "col", 0)
    pivot_block = lax.psum(
        row_pick(panel_l, col_index * blocks, row_index, rows_axis, blocks), "row"
    )
    update = jnp.einsum("qrt,jt->qrj", panel_l, pivot_block, precision=lax.Precision.HIGHEST)
    current = jnp.where(col_index >= 0, current - update, current)
    replace = (col_index == 0) & (active[None, None, :] > 0)
    current = jnp.where(replace, panel_l, current)
    factored = jnp.where(keep_mask, current, jnp.zeros_like(current))
    return factored[None]


def solution(mesh):
    in_specs = (
        P("front", None, "row", "col"),
        P("front", None, "row", "col"),
        P(),
        P(),
        P("front"),
        P("front"),
    )
    out_specs = P("front", None, "row", "col")
    return jax.shard_map(
        on_device, mesh=mesh, in_specs=in_specs, out_specs=out_specs, check_vma=False
    )
```

profile of v0, /device:TPU:1, one launch (start us, length us, event | category | flops | bytes accessed | tf_op | source)
XLA Modules:
  0.0 616.1 jit_solution(13606290763612168228)
XLA Ops:
  6.5 0.0 copy-start
  6.5 0.0 all-gather.2.cloned.1.call-start
  6.5 4.7 copy.75
  11.2 0.0 all-gather.2.cloned.1.call-update
  11.2 0.0 all-reduce.5.cloned.1.call-start
  11.3 0.1 copy.54
  11.5 0.1 reshape.216
  12.3 0.1 fusion.19
  12.4 0.1 iota_add_fusion
  12.4 235.6 %all-gather.2.cloned.1.call-done = f32[64,4,128,256]{3,2,1,0:T(8,128)} async-done(((f32[2,4,128,256]{3,2,1,0:T(8,128)}), f32[64,4,128,256]{3,2,1,0:T(8,128)}) %all-gather.2.cloned.1.call-update) | async-done | bytes 33554448 | tf_op jit(solution)/shard_map/all_gather | solution.py:58
  248.1 23.2 %broadcast_multiply_fusion = f32[64,4,128,256]{3,2,1,0:T(8,128)} fusion(f32[64,4,128,256]{3,2,1,0:T(8,128)} %all-gather.2.cloned.1.call-done, f32[64]{0:T(128)S(1)} %compare_convert_fusion), kind=kLoop, calls=%fused_computation.3 | loop fusion | flops 8388608 | bytes 67109120 | tf_op jit(solution)/shard_map/mul | solution.py:64
  271.3 73.8 %scatter_fusion = f32[32,128,256]{2,1,0:T(8,128)} fusion(f32[32,128,256]{2,1,0:T(8,128)} %bitcast.69, s32[256]{0:T(256)S(1)} %reshape.216, f32[256,128,256]{2,1,0:T(8,128)} %bitcast.70), kind=kCustom, calls=%fused_computation | custom fusion | flops 8388608 | bytes 100664320 | tf_op jit(solution)/shard_map/scatter-add | solution.py:64
  345.1 5.6 copy.35
  350.7 3.0 fusion.3
  353.7 0.0 copy-start.2
  353.7 2.0 copy-done.2
  355.8 0.7 pad_maximum_fusion.1
  356.5 0.0 all-reduce.5.cloned.1.call-update
  356.5 0.2 all-reduce.7.cloned.1.call-start
  357.4 41.3 %all-reduce.5.cloned.1.call-done = f32[256,256]{0,1:T(8,128)} async-done(((f32[256,256]{0,1:T(8,128)}), f32[256,256]{0,1:T(8,128)}) %all-reduce.5.cloned.1.call-update) | async-done | bytes 262160 | tf_op jit(solution)/shard_map/psum | solution.py:74
  398.7 1.0 select_bitcast_fusion
  399.7 0.1 copy.36
  399.8 1.1 select_add_fusion
  400.9 0.1 copy.38
  401.1 11.7 %cholesky.49 = f32[128,128]{1,0:T(8,128)S(1)} custom-call(f32[128,128]{1,0:T(8,128)S(1)} %cholesky.115), custom_call_target="Cholesky" | custom-call | tf_op jit(solution)/shard_map/jit(cholesky)/cholesky | solution.py:29
  412.8 9.8 %custom-call.14 = f32[1,128,128]{1,2,0:T(8,128)S(1)} custom-call(f32[1,128,128]{2,1,0:T(8,128)S(1)} %get-tuple-element.66), custom_call_target="InvertDiagBlocksLowerTriangular" | custom-call | tf_op jit(solution)/shard_map/jit(cholesky)/cholesky | solution.py:29
  422.6 0.2 fusion.14
  422.9 0.3 convolution_subtract_fusion.1
  423.1 11.7 %cholesky.103 = f32[128,128]{1,0:T(8,128)S(1)} custom-call(f32[128,128]{1,0:T(8,128)S(1)} %convolution_subtract_fusion.1), custom_call_target="Cholesky" | custom-call | tf_op jit(solution)/shard_map/jit(cholesky)/cholesky | solution.py:29
  434.9 0.1 copy.41
  435.0 0.1 copy.40
  435.1 0.1 copy.39
  435.2 0.7 compare_reduce_fusion
  437.3 0.1 triangular_solve.43
  437.3 4.5 while.3
  437.5 0.7 fusion.29
  438.2 1.3 dynamic-slice.23
  439.5 0.1 copy.56
  439.7 0.7 fusion.29
  440.3 1.3 dynamic-slice.23
  441.7 0.1 copy.56
  441.8 19.7 %custom-call.15 = f32[2,128,128]{1,2,0:T(8,128)S(1)} custom-call(f32[2,128,128]{2,1,0:T(8,128)S(1)} %get-tuple-element.36), custom_call_target="InvertDiagBlocksLowerTriangular" | custom-call | tf_op jit(solution)/shard_map/triangular_solve | solution.py:41
  461.5 0.9 slice_select_fusion.1
  462.4 0.7 bitcast_dynamic-update-slice_fusion.1
  463.1 0.7 fusion.9
  463.8 4.8 broadcast_multiply_fusion.1
  468.6 5.6 copy.37
  474.2 3.7 fusion.4
  478.0 0.0 copy-done.3
  478.0 3.4 convolution_subtract_fusion
  481.4 2.0 fusion.12
  483.4 2.5 pad_maximum_fusion
  485.9 5.6 copy.43
  491.5 5.6 copy.44
  497.1 4.9 select_select_fusion
  502.0 0.0 all-reduce.7.cloned.1.call-update
  502.0 0.0 all-reduce.9.cloned.1.call-start
  502.1 42.6 %all-reduce.7.cloned.1.call-done = f32[32,128,256]{1,2,0:T(8,128)} async-done(((f32[32,128,256]{1,2,0:T(8,128)}), f32[32,128,256]{1,2,0:T(8,128)}) %all-reduce.7.cloned.1.call-update) | async-done | bytes 4194320 | tf_op jit(solution)/shard_map/psum | solution.py:9
  544.7 1.0 select_bitcast_fusion.2
  545.7 0.7 pad_maximum_fusion.2
  546.4 0.0 all-reduce.9.cloned.1.call-update
  546.5 45.7 %all-reduce.9.cloned.1.call-done = f32[256,256]{0,1:T(8,128)} async-done(((f32[256,256]{0,1:T(8,128)}), f32[256,256]{0,1:T(8,128)}) %all-reduce.9.cloned.1.call-update) | async-done | bytes 262160 | tf_op jit(solution)/shard_map/psum | solution.py:77
  592.2 11.8 %fusion.2 = f32[1,32,128,256]{2,3,1,0:T(8,128)} fusion(f32[32,128,256]{1,2,0:T(8,128)} %all-reduce.7.cloned.1.call-done, s32[32,128]{1,0:T(8,128)S(1)} %iota_add_fusion, s32[256]{0:T(256)S(1)} %iota_add_fusion.2, pred[256]{0:T(512)(128)(4,1)S(1)} %compare_and_fusion.1, pred[]{:T(512)S(6)} %ge.48, pred[32,128]{1,0:T(8,128)(4,1)S(1)} %get-tuple-element.68, ...), kind=kOutput, calls=%fused_computation.8 | convolution fusion | flops 3228565504 | bytes 12866817 | tf_op jit(solution)/shard_map/qrt,jt->qrj/dot_general | solution.py:80
  603.9 5.6 copy.48
  (30 shorter events, 0.3 us)
Async XLA Ops:
  6.5 4.8 copy-start
  6.5 5.7 copy-start.4
  6.5 241.5 %all-gather.2.cloned.1.call-start = ((), (), s32[]{:S(2)}) async-start(), calls=%async_computation | async-start | bytes 34603008 | tf_op jit(solution)/shard_map/all_gather | solution.py:58
  11.2 387.5 %all-reduce.5.cloned.1.call-start = ((), (), s32[]{:S(2)}) async-start(), calls=%async_computation.1 | async-start | bytes 524288 | tf_op jit(solution)/shard_map/psum | solution.py:74
  353.7 2.0 copy-start.2
  356.5 188.2 %all-reduce.7.cloned.1.call-start = ((), (), s32[]{:S(2)}) async-start(), calls=%async_computation.2 | async-start | bytes 8388608 | tf_op jit(solution)/shard_map/psum | solution.py:9
  474.2 3.8 copy-start.3
  502.0 90.2 %all-reduce.9.cloned.1.call-start = ((), (), s32[]{:S(2)}) async-start(), calls=%async_computation.3 | async-start | bytes 524288 | tf_op jit(solution)/shard_map/psum | solution.py:77
  592.2 17.4 %copy-start.1 = (s32[64,16]{0,1:T(8,128)S(1)}, s32[64,16]{0,1:T(8,128)}, u32[]{:S(2)}) copy-start(s32[64,16]{0,1:T(8,128)} %param.13) | copy-start | bytes 12292
Sparse Core Ops, SparseCore 0:
  11.4 236.6 all-gather.1
  356.6 42.0 all-reduce.4
  502.1 42.5 all-reduce.6
  546.9 45.2 all-reduce.8
where the time goes:
time: 618 us; the launch traced here: 616 us
  waiting for transfers between devices  365 us (59%)
  other arithmetic  172 us (28%)
  local copies, waits for them, and re-layouts  40.4 us (7%)
  matrix products  21.4 us (3%)
  between operations  16 us (3%)
    all_gather x1, waiting for transfers between devices, on_device(): pieces = lax.all_gather(children, 'front', axis=0, tiled=True)  236 us
    scatter-add x1, other arithmetic, on_device(): current = current.at[target].add(pieces * owned_mask[:, None, None, None])  73.8 us
    psum x1, waiting for transfers between devices, on_device(): lax.psum(row_pick(panel_l, col_index * blocks, row_index, rows_axis, bloc...  45.7 us
    psum x1, waiting for transfers between devices, broadcast(): return lax.psum(jnp.where(mine, value, jnp.zeros_like(value)), axis)  42.6 us
    psum x1, waiting for transfers between devices, on_device(): lax.psum(row_pick(current, 0 * blocks, row_index, rows_axis, blocks), 'row')  41.3 us
    another operation x6, other arithmetic, factor_panel(): factor = jnp.linalg.cholesky(masked)  34 us
    mul x1, other arithmetic, on_device(): current = current.at[target].add(pieces * owned_mask[:, None, None, None])  23.2 us
    another operation x4, other arithmetic, factor_panel(): lax.linalg.triangular_solve(factor, flat_rows, left_side=False, lower=Tru...  22.2 us
  transfers between devices with their start and end apart: 4, of which 4 were waited for; matrix products, arithmetic and copies ran while one was open for 0% of the time, Pallas kernels for 0%

commit v1 on v0

v1 whole, which is shorter than its diff:
```python
import jax
import jax.numpy as jnp
from jax import lax
from jax.experimental import pallas as pl
from jax.experimental.pallas import tpu as pltpu
from jax.sharding import PartitionSpec as P

F32 = jnp.float32
BLOCK = 128
WIDTH = 256
BASE = 32
VMEM = pl.BlockSpec(memory_space=pltpu.VMEM)
SMEM = pl.BlockSpec(memory_space=pltpu.SMEM)


def dot(a, b, ca=1, cb=0):
    return lax.dot_general(
        a, b, (((ca,), (cb,)), ((), ())),
        precision=lax.Precision.HIGHEST, preferred_element_type=F32,
    )


def targets_of(maps_ref, child, row, rows):
    cycles = maps_ref.shape[1] // rows
    targets = [maps_ref[child, rows * i + row] // rows for i in range(cycles)]
    first = jnp.int32(0)
    found = jnp.int32(0)
    for i in range(cycles):
        hit = targets[i] == 0
        first = jnp.where(hit, i, first)
        found = jnp.where(hit, 1, found)
    return targets, first, found


def slot_block(slot, first):
    if slot == 0:
        return first
    return jnp.where(first >= slot, slot - 1, slot)


def pick(values, at):
    out = values[0]
    for i in range(1, len(values)):
        out = jnp.where(at == i, values[i], out)
    return out


def child_of(parents_ref, front, which):
    found = jnp.int32(0)
    for d in range(parents_ref.shape[0] // 2):
        found = jnp.where(parents_ref[2 * d + which] == front, 2 * d + which, found)
    return found


def spread_kernel(maps_ref, children_ref, out_ref, *, rows):
    front, row = lax.axis_index("front"), lax.axis_index("row")
    cycles = children_ref.shape[1]
    for c in range(2):
        _, first, _ = targets_of(maps_ref, 2 * front + c, row, rows)
        for s in range(cycles):
            block = slot_block(s, first)
            at = (c * cycles + s) * 8
            for half in range(2):
                tiles = children_ref[c, block, :, half * 128:(half + 1) * 128]
                out_ref[:, half, at:at + 8, :] = tiles.reshape(BLOCK // 8, 8, 128)


def route_kernel(parents_ref, in_ref, first_ref, rest_ref):
    fronts, depth = in_ref.shape[0], in_ref.shape[1]
    half = depth // 2
    for d in range(fronts):
        for c in range(2):
            to = parents_ref[2 * d + c]
            first_ref[to, c * 8:(c + 1) * 8, :] = in_ref[d, c * half:c * half + 8, :]
            rest_ref[to, c * (half - 8):(c + 1) * (half - 8), :] = in_ref[
                d, c * half + 8:(c + 1) * half, :
            ]


def tile_block(ref, at):
    return jnp.concatenate(
        [ref[:, half, at:at + 8, :].reshape(BLOCK, 128) for half in range(2)], axis=1
    )


def top_kernel(parents_ref, maps_ref, panel_ref, first_ref, out_ref, *, rows):
    front, row = lax.axis_index("front"), lax.axis_index("row")
    total = panel_ref[0]
    for c in range(2):
        child = child_of(parents_ref, front, c)
        _, _, found = targets_of(maps_ref, child, row, rows)
        total = total + tile_block(first_ref, c * 8) * found.astype(F32)
    out_ref[...] = total


def invert_base(a):
    n = a.shape[0]
    r = lax.broadcasted_iota(jnp.int32, (n, n), 0)
    l = lax.broadcasted_iota(jnp.int32, (n, n), 1)
    t = jnp.where(r == l, 1.0, 0.0).astype(F32)
    rows = lax.broadcasted_iota(jnp.int32, (n, 1), 0)
    for j in range(n - 1):
        f = jnp.where(rows > j, a[:, j:j + 1] / a[j:j + 1, j:j + 1], 0.0)
        a = a - f * a[j:j + 1, :]
        t = t - f * t[j:j + 1, :]
    d = jnp.sum(jnp.where(r == l, a, 0.0), axis=1, keepdims=True)
    return t * lax.rsqrt(d)


def invert_factor(a):
    n = a.shape[0]
    if n == BASE:
        return invert_base(a)
    h = n // 2
    w1 = invert_factor(a[:h, :h])
    l21 = dot(a[h:, :h], w1, 1, 1)
    w2 = invert_factor(a[h:, h:] - dot(l21, l21, 1, 1))
    w21 = -dot(w2, dot(l21, w1))
    return jnp.concatenate(
        [
            jnp.concatenate([w1, jnp.zeros((h, h), F32)], axis=1),
            jnp.concatenate([w21, w2], axis=1),
        ],
        axis=0,
    )


def factor_kernel(pivots_ref, own_ref, r1_ref, r2_ref, r3_ref, solve_ref, send_ref, all_ref):
    row = lax.axis_index("row")
    for s, ref in enumerate((own_ref, r1_ref, r2_ref, r3_ref)):
        at = pl.multiple_of(lax.rem(row + 4 - s, 4) * BLOCK, BLOCK)
        all_ref[pl.ds(at, BLOCK), :] = ref[...]
    pivots = pivots_ref[0]
    r = lax.broadcasted_iota(jnp.int32, (WIDTH, WIDTH), 0)
    l = lax.broadcasted_iota(jnp.int32, (WIDTH, WIDTH), 1)
    both = (r < pivots) & (l < pivots)
    diag = all_ref[0:WIDTH, :]
    low = jnp.where(r >= l, diag, 0.0)
    strict = jnp.where(r > l, diag, 0.0)
    mirrored = low + strict.T
    masked = jnp.where(both, mirrored, jnp.where(r == l, 1.0, 0.0))
    inverse = jnp.where(both, invert_factor(masked), 0.0)
    solved = dot(all_ref[...], inverse, 1, 1)
    top = jnp.where(r >= l, solved[:WIDTH], 0.0)
    solve_t = inverse - jnp.where(r < pivots, 0.0, dot(top, inverse))
    update_t = dot(solved[WIDTH:], inverse)
    solve_ref[...] = solve_t.T
    send_ref[0:WIDTH, :] = update_t.T
    send_ref[WIDTH:, :] = own_ref[...]


def main_kernel(orders_ref, pivots_ref, panel_ref, left_ref, top_ref, solve_ref, sent_ref, out_ref, *, rows):
    row, col = lax.axis_index("row"), lax.axis_index("col")
    step = pl.program_id(0)
    cycles = panel_ref.shape[0]
    orders, pivots = orders_ref[0], pivots_ref[0]
    lane = lax.broadcasted_iota(jnp.int32, (1, WIDTH), 1)
    rest = jnp.where(lane < pivots, 0.0, 1.0)
    first = step == 0
    x0 = jnp.where(first, top_ref[...], panel_ref[0])

    @pl.when(col == 0)
    def _():
        x = jnp.concatenate([x0] + [panel_ref[i] for i in range(1, cycles)], axis=0)
        y = dot(x, solve_ref[...]) + x * rest
        for i in range(cycles):
            out_ref[i] = y[i * BLOCK:(i + 1) * BLOCK]

    @pl.when(col != 0)
    def _():
        z0 = jnp.where(first, sent_ref[WIDTH:, :], left_ref[0])
        x = jnp.concatenate([z0] + [left_ref[i] for i in range(1, cycles)], axis=0)
        y = dot(x, sent_ref[0:WIDTH, :])
        out_ref[0] = x0 - y[:BLOCK]
        for i in range(1, cycles):
            out_ref[i] = panel_ref[i] - y[i * BLOCK:(i + 1) * BLOCK]

    for i in range(cycles):
        start = ((step * cycles + i) * rows + row) * BLOCK

        @pl.when(start >= orders)
        def _():
            out_ref[i] = jnp.zeros((BLOCK, WIDTH), F32)

    @pl.when(first)
    def _():
        g = row * BLOCK + lax.broadcasted_iota(jnp.int32, (BLOCK, WIDTH), 0)
        j = col * WIDTH + lax.broadcasted_iota(jnp.int32, (BLOCK, WIDTH), 1)
        out_ref[0] = jnp.where(g >= j, out_ref[0], 0.0)


def late_kernel(parents_ref, maps_ref, pivots_ref, first_ref, rest_ref, lfirst_ref, lrest_ref,
                solve_ref, sent_ref, base_ref, out_ref, hold_ref, sem_in, sem_out, *, rows):
    front, row, col = lax.axis_index("front"), lax.axis_index("row"), lax.axis_index("col")
    cycles = maps_ref.shape[1] // rows
    pivots = pivots_ref[0]
    lane = lax.broadcasted_iota(jnp.int32, (1, WIDTH), 1)
    rest = jnp.where(lane < pivots, 0.0, 1.0)
    for c in range(2):
        child = child_of(parents_ref, front, c)
        targets, first, found = targets_of(maps_ref, child, row, rows)
        place = [pick(targets, slot_block(s, first)) for s in range(cycles)]
        for s in range(cycles):
            @pl.when(place[s] != 0)
            def _():
                pltpu.make_async_copy(base_ref.at[place[s]], hold_ref.at[s], sem_in.at[s]).start()
        for s in range(cycles):
            at = c * 8 if s == 0 else (c * (cycles - 1) + s - 1) * 8
            mine, left = (first_ref, lfirst_ref) if s == 0 else (rest_ref, lrest_ref)

            @pl.when(place[s] != 0)
            def _():
                pltpu.make_async_copy(base_ref.at[place[s]], hold_ref.at[s], sem_in.at[s]).wait()

                @pl.when(col == 0)
                def _():
                    x = tile_block(mine, at)
                    hold_ref[s] = hold_ref[s] + x * rest + dot(x, solve_ref[...])

                @pl.when(col != 0)
                def _():
                    hold_ref[s] = hold_ref[s] + tile_block(mine, at) - dot(
                        tile_block(left, at), sent_ref[0:WIDTH, :]
                    )

                pltpu.make_async_copy(hold_ref.at[s], out_ref.at[place[s]], sem_out.at[s]).start()
        for s in range(cycles):
            @pl.when(place[s] != 0)
            def _():
                pltpu.make_async_copy(hold_ref.at[s], out_ref.at[place[s]], sem_out.at[s]).wait()


def on_device(panel, children, parents, row_maps, orders, pivots):
    rows = lax.axis_size("row")
    fronts = lax.axis_size("front")
    cycles = panel.shape[1]
    child_cycles = children.shape[1]
    panel = panel[0]
    depth = 2 * child_cycles * 8
    params = pltpu.CompilerParams(vmem_limit_bytes=40 * 2**20)

    to_right = [(0, 1)]
    left = lax.ppermute(panel, "col", to_right)

    spread = pl.pallas_call(
        lambda *refs: spread_kernel(*refs, rows=rows),
        out_shape=jax.ShapeDtypeStruct((BLOCK // 8, 2, depth, 128), F32),
        in_specs=[SMEM, VMEM], out_specs=VMEM, compiler_params=params, name="spread",
    )(row_maps, children)
    spread = lax.all_to_all(spread.reshape(fronts, depth, 128), "front", 0, 0, tiled=True)
    first, rest = pl.pallas_call(
        route_kernel,
        out_shape=(
            jax.ShapeDtypeStruct((fronts, 16, 128), F32),
            jax.ShapeDtypeStruct((fronts, depth - 16, 128), F32),
        ),
        in_specs=[SMEM, VMEM], out_specs=(VMEM, VMEM), compiler_params=params, name="route",
    )(parents, spread)
    first = lax.all_to_all(first, "front", 0, 0, tiled=True)
    rest, first = lax.optimization_barrier((rest, first))
    rest = lax.all_to_all(rest, "front", 0, 0, tiled=True)
    pieces = (BLOCK // 8, 2)
    first = first.reshape(*pieces, 16, 128)
    rest = rest.reshape(*pieces, depth - 16, 128)

    top = pl.pallas_call(
        lambda *refs: top_kernel(*refs, rows=rows),
        grid=(1,),
        out_shape=jax.ShapeDtypeStruct((BLOCK, WIDTH), F32),
        in_specs=[
            SMEM, SMEM,
            pl.BlockSpec((1, BLOCK, WIDTH), lambda i: (0, 0, 0)),
            pl.BlockSpec((*pieces, 16, 128), lambda i: (0, 0, 0, 0)),
        ],
        out_specs=pl.BlockSpec((BLOCK, WIDTH), lambda i: (0, 0)),
        compiler_params=params, name="top",
    )(parents, row_maps, panel, first)
    others = [
        lax.ppermute(top, "row", [(i, (i + s) % rows) for i in range(rows)]) for s in (1, 2, 3)
    ]
    solve, send = pl.pallas_call(
        factor_kernel,
        out_shape=(
            jax.ShapeDtypeStruct((WIDTH, WIDTH), F32),
            jax.ShapeDtypeStruct((WIDTH + BLOCK, WIDTH), F32),
        ),
        in_specs=[SMEM, VMEM, VMEM, VMEM, VMEM], out_specs=(VMEM, VMEM),
        scratch_shapes=[pltpu.VMEM((4 * BLOCK, WIDTH), F32)],
        compiler_params=params, name="factor",
        cost_estimate=pl.CostEstimate(flops=2 * 10**9, bytes_accessed=2**21, transcendentals=0),
    )(pivots, top, *others)
    sent = lax.ppermute(send, "col", to_right)
    left_first = lax.ppermute(first, "col", to_right)

    per = 4
    chunk = pl.BlockSpec((per, BLOCK, WIDTH), lambda i: (i, 0, 0))
    whole = lambda *shape: pl.BlockSpec(shape, lambda i: (0,) * len(shape))
    base = pl.pallas_call(
        lambda *refs: main_kernel(*refs, rows=rows),
        grid=(cycles // per,),
        out_shape=jax.ShapeDtypeStruct(panel.shape, F32),
        in_specs=[
            SMEM, SMEM, chunk, chunk,
            whole(BLOCK, WIDTH), whole(WIDTH, WIDTH), whole(WIDTH + BLOCK, WIDTH),
        ],
        out_specs=chunk, compiler_params=params, name="main",
        cost_estimate=pl.CostEstimate(flops=10**9, bytes_accessed=12 * 2**20, transcendentals=0),
    )(orders, pivots, panel, left, top, solve, sent)

    left_rest = lax.ppermute(rest, "col", to_right)
    hbm = pl.BlockSpec(memory_space=pl.ANY)
    out = pl.pallas_call(
        lambda *refs: late_kernel(*refs, rows=rows),
        out_shape=jax.ShapeDtypeStruct(panel.shape, F32),
        in_specs=[SMEM, SMEM, SMEM, VMEM, VMEM, VMEM, VMEM, VMEM, VMEM, hbm],
        out_specs=hbm,
        scratch_shapes=[
            pltpu.VMEM((child_cycles, BLOCK, WIDTH), F32),
            pltpu.SemaphoreType.DMA((child_cycles,)),
            pltpu.SemaphoreType.DMA((child_cycles,)),
        ],
        input_output_aliases={9: 0},
        compiler_params=params, name="late",
        cost_estimate=pl.CostEstimate(flops=10**8, bytes_accessed=4 * 2**20, transcendentals=0),
    )(parents, row_maps, pivots, first, rest, left_first, left_rest, solve, sent, base)
    return out[None]


def solution(mesh):
    in_specs = (
        P("front", None, "row", "col"),
        P("front", None, "row", "col"),
        P(),
        P(),
        P("front"),
        P("front"),
    )
    out_specs = P("front", None, "row", "col")
    return jax.shard_map(
        on_device, mesh=mesh, in_specs=in_specs, out_specs=out_specs, check_vma=False
    )
```

time: 618 us -> 137 us (0.22)
  waiting for transfers between devices: 365 us -> 39.6 us
  other arithmetic: 172 us -> 0 us
  Pallas kernels: 0 us -> 47.8 us
  local copies, waits for them, and re-layouts: 40.4 us -> 4.21 us
  starting transfers between devices: 0.31 us -> 26.5 us
  matrix products: 21.4 us -> 0 us
  blocking collectives: 0 us -> 16.5 us
  between operations: 16 us -> 1.56 us
    all_gather x1 -> x0, waiting for transfers between devices: 236 us -> none  [on_device(): pieces = lax.all_gather(children, 'front', axis=0, tiled=True)]
    psum x3 -> x0, waiting for transfers between devices: 130 us -> none  [the longest x1 45.7 us: on_device(): lax.psum(row_pick(panel_l, col_index * blocks, row_index, rows_axis, bloc...]
    scatter-add x1 -> x0, other arithmetic: 73.8 us -> none  [on_device(): current = current.at[target].add(pieces * owned_mask[:, None, None, None])]
    another operation x10 -> x0, other arithmetic: 56.2 us -> none  [the longest x6 34 us: factor_panel(): factor = jnp.linalg.cholesky(masked)]
    pallas_call x0 -> x6, Pallas kernels: none -> 47.8 us  [the longest x1 27.6 us: on_device(): pl.pallas_call(factor_kernel, out_shape=(jax.ShapeDtypeStruct((WIDTH, WID...]
    all_to_all x0 -> x2, waiting for transfers between devices: none -> 34.4 us  [the longest x1 24.9 us: on_device(): lax.all_to_all(spread.reshape(fronts, depth, 128), 'front', 0, 0, tiled=T...]
    mul x3 -> x0, other arithmetic: 28.1 us -> none  [the longest x1 23.2 us: on_device(): current = current.at[target].add(pieces * owned_mask[:, None, None, None])]
    all_to_all x0 -> x1, blocking collectives: none -> 16.5 us  [on_device(): first = lax.all_to_all(first, 'front', 0, 0, tiled=True)]
  transfers between devices with their start and end apart: 4 -> 9, of which waited for: 4 -> 3; matrix products, arithmetic and copies ran while one was open for 0% -> 0% of each run, Pallas kernels for 0% -> 29%
where the time goes in v1:
time: 137 us; the launch traced here: 136 us
  Pallas kernels  47.8 us (35%)
  waiting for transfers between devices  39.6 us (29%)
  starting transfers between devices  26.5 us (19%)
  blocking collectives  16.5 us (12%)
  local copies, waits for them, and re-layouts  4.21 us (3%)
  between operations  1.56 us (1%)
    pallas_call x1, Pallas kernels, on_device(): pl.pallas_call(factor_kernel, out_shape=(jax.ShapeDtypeStruct((WIDTH, WID...  27.6 us
    all_to_all x1, waiting for transfers between devices, on_device(): lax.all_to_all(spread.reshape(fronts, depth, 128), 'front', 0, 0, tiled=T...  24.9 us
    all_to_all x1, blocking collectives, on_device(): first = lax.all_to_all(first, 'front', 0, 0, tiled=True)  16.5 us
    all_to_all x1, starting transfers between devices, on_device(): lax.all_to_all(spread.reshape(fronts, depth, 128), 'front', 0, 0, tiled=T...  11.9 us
    all_to_all x1, waiting for transfers between devices, on_device(): rest = lax.all_to_all(rest, 'front', 0, 0, tiled=True)  9.46 us
    pallas_call x1, Pallas kernels, on_device(): pl.pallas_call(lambda *refs: main_kernel(*refs, rows=rows), grid=(cycles...  8.96 us
    pallas_call x1, Pallas kernels, on_device(): pl.pallas_call(lambda *refs: late_kernel(*refs, rows=rows), out_shape=jax...  6.3 us
    ppermute x1, waiting for transfers between devices, on_device(): sent = lax.ppermute(send, 'col', to_right)  5.25 us
  transfers between devices with their start and end apart: 9, of which 3 were waited for; matrix products, arithmetic and copies ran while one was open for 0% of the time, Pallas kernels for 29%

profile of v1, /device:TPU:1, one launch (start us, length us, event | category | flops | bytes accessed | tf_op | source)
XLA Modules:
  0.0 136.2 jit_solution(8861101103500939690)
XLA Ops:
  0.0 0.0 copy-start.3
  0.0 0.8 copy.10.refs_0_.refs_1_
  0.8 0.0 copy-start.2
  0.8 1.2 copy-done.2
  2.0 2.2 %spread.1 = f32[16,2,64,128]{3,2,1,0:T(8,128)} custom-call(s32[64,16]{1,0:T(8,128)S(1)} %copy.10.refs_0_.refs_1_, f32[2,4,128,256]{3,2,1,0:T(8,128)S(1)} %copy-done.2), custom_call_target="tpu_custom_call" | custom-call | tf_op jit(solution)/shard_map/spread/pallas_call | solution.py:245
  4.2 11.9 %all-to-all-start = ((f32[32,64,128]{2,1,0:T(8,128)}), f32[32,64,128]{2,1,0:T(8,128)S(1)}, u32[]{:S(2)}, u32[]{:S(2)}) async-start(f32[32,64,128]{2,1,0:T(8,128)} %bitcast), calls=%async_computation | async-start | bytes 2097152 | tf_op jit(solution)/shard_map/all_to_all | solution.py:250
  16.1 1.3 collective-permute-start.6
  17.4 24.9 %all-to-all-done.in_ref = f32[32,64,128]{2,1,0:T(8,128)S(1)} async-done(((f32[32,64,128]{2,1,0:T(8,128)}), f32[32,64,128]{2,1,0:T(8,128)S(1)}, u32[]{:S(2)}, u32[]{:S(2)}) %all-to-all-start) | async-done | bytes 1048608 | tf_op jit(solution)/shard_map/all_to_all | solution.py:250
  42.3 0.0 copy-done.3
  42.3 1.5 %route.1 = (f32[32,16,128]{2,1,0:T(8,128)S(1)}, f32[32,48,128]{2,1,0:T(8,128)}) custom-call(s32[64]{0:T(128)S(1)} %copy-done.3, f32[32,64,128]{2,1,0:T(8,128)S(1)} %all-to-all-done.in_ref), custom_call_target="tpu_custom_call" | custom-call | tf_op jit(solution)/shard_map/route/pallas_call | solution.py:251
  43.8 16.5 %all_to_all.15 = f32[32,16,128]{2,1,0:T(8,128)S(1)} all-to-all(f32[32,16,128]{2,1,0:T(8,128)S(1)} %get-tuple-element.12), channel_id=1, replica_groups=mesh['front'=32,'row'=4,'col'=2] {'front'}, dimensions={0} | all-to-all | bytes 524288 | tf_op jit(solution)/shard_map/all_to_all | solution.py:259
  60.4 4.0 %all-to-all-start.2 = ((f32[32,48,128]{2,1,0:T(8,128)}), f32[32,48,128]{2,1,0:T(8,128)S(1)}, u32[]{:S(2)}, u32[]{:S(2)}) async-start(f32[32,48,128]{2,1,0:T(8,128)} %get-tuple-element.14), calls=%async_computation.2 | async-start | bytes 1572864 | tf_op jit(solution)/shard_map/all_to_all | solution.py:261
  64.4 0.0 copy-start
  64.4 2.2 %copy-done = f32[1,32,128,256]{3,2,1,0:T(8,128)S(1)} copy-done((f32[1,32,128,256]{3,2,1,0:T(8,128)S(1)}, f32[1,32,128,256]{3,2,1,0:T(8,128)}, u32[]{:S(2)}) %copy-start) | copy-done | bytes 4194328
  66.5 1.2 top.1.own_ref.refs_4_
  67.8 1.4 %collective-permute-start.2 = (f32[128,256]{1,0:T(8,128)S(1)}, f32[128,256]{1,0:T(8,128)S(1)}, u32[]{:S(2)}, u32[]{:S(2)}) collective-permute-start(f32[128,256]{1,0:T(8,128)S(1)} %top.1.own_ref.refs_4_), channel_id=1, source_target_pairs={{0,2},{2,4},{4,6},{6,0},{1,3},{3,5},{5,7},{7,1},{8,10},{10,12},{12... | collective-permute-start | bytes 393224 | tf_op jit(solution)/shard_map/ppermute | solution.py:279
  69.1 2.6 %collective-permute-start.3 = (f32[128,256]{1,0:T(8,128)S(1)}, f32[128,256]{1,0:T(8,128)S(1)}, u32[]{:S(2)}, u32[]{:S(2)}) collective-permute-start(f32[128,256]{1,0:T(8,128)S(1)} %top.1.own_ref.refs_4_), channel_id=1, source_target_pairs={{0,4},{2,6},{4,0},{6,2},{1,5},{3,7},{5,1},{7,3},{8,12},{10,14},{12... | collective-permute-start | bytes 393224 | tf_op jit(solution)/shard_map/ppermute | solution.py:279
  71.7 1.1 collective-permute-start.4
  72.8 9.5 %all-to-all-done.2 = f32[32,48,128]{2,1,0:T(8,128)S(1)} async-done(((f32[32,48,128]{2,1,0:T(8,128)}), f32[32,48,128]{2,1,0:T(8,128)S(1)}, u32[]{:S(2)}, u32[]{:S(2)}) %all-to-all-start.2) | async-done | bytes 786464 | tf_op jit(solution)/shard_map/all_to_all | solution.py:261
  82.3 0.0 copy-start.1
  82.3 1.5 %collective-permute-start.1 = (f32[16,2,48,128]{3,2,1,0:T(8,128)S(1)}, f32[16,2,48,128]{3,2,1,0:T(8,128)S(1)}, u32[]{:S(2)}, u32[]{:S(2)}) collective-permute-start(f32[16,2,48,128]{3,2,1,0:T(8,128)S(1)} %bitcast.8), channel_id=1, source_target_pairs={{0,1},{2,3},{4,5},{6,7},{8,9},{10,11},{12,13},{14,15},{16,17},{18,... | collective-permute-start | bytes 2359304 | tf_op jit(solution)/shard_map/ppermute | solution.py:310
  84.5 0.0 collective-permute-done.2.r1_ref
  84.5 0.0 collective-permute-done.3.r2_ref
  84.5 0.0 collective-permute-done.4.r3_ref
  84.5 27.6 %factor.1 = (f32[256,256]{1,0:T(8,128)S(1)}, f32[384,256]{1,0:T(8,128)S(1)}) custom-call(s32[1]{0:T(128)S(6)} %copy.13.pivots_ref.refs_1_.refs_2_, f32[128,256]{1,0:T(8,128)S(1)} %top.1.own_ref.refs_4_, f32[128,256]{1,0:T(8,128)S(1)} %collective-permute-done.2.r1_ref, f32[128,256]{1,0:T(8,128)S(1)} %collective-permute-done.3.r2_ref, ...), custom_call_target="tpu_custom_call" | custom-call | flops 2000000000 | bytes 2097152 | tf_op jit(solution)/shard_map/factor/pallas_call | solution.py:281
  112.1 1.3 collective-permute-start.5
  113.4 1.5 %collective-permute-start = (f32[16,2,16,128]{3,2,1,0:T(8,128)S(1)}, f32[16,2,16,128]{3,2,1,0:T(8,128)S(1)}, u32[]{:S(2)}, u32[]{:S(2)}) collective-permute-start(f32[16,2,16,128]{3,2,1,0:T(8,128)S(1)} %bitcast.11), channel_id=1, source_target_pairs={{0,1},{2,3},{4,5},{6,7},{8,9},{10,11},{12,13},{14,15},{16,17},{18,... | collective-permute-start | bytes 786440 | tf_op jit(solution)/shard_map/ppermute | solution.py:293
  115.5 5.3 %collective-permute-done.5.refs_6_.refs_8_ = f32[384,256]{1,0:T(8,128)S(1)} collective-permute-done((f32[384,256]{1,0:T(8,128)S(1)}, f32[384,256]{1,0:T(8,128)S(1)}, u32[]{:S(2)}, u32[]{:S(2)}) %collective-permute-start.5) | collective-permute-done | bytes 393248 | tf_op jit(solution)/shard_map/ppermute | solution.py:292
  120.8 0.0 collective-permute-done.6.refs_3_
  120.8 0.0 copy-done.1
  120.8 9.0 %main.1.refs_9_ = f32[32,128,256]{2,1,0:T(8,128)} custom-call(s32[1]{0:T(128)S(6)} %copy.12.refs_0_, s32[1]{0:T(128)S(6)} %copy.13.pivots_ref.refs_1_.refs_2_, f32[32,128,256]{2,1,0:T(8,128)S(1)} %bitcast.7, f32[32,128,256]{2,1,0:T(8,128)} %collective-permute-done.6.refs_3_, f32[128,256]{1,0:T(8,128)S(1)} %top.1.own_ref.refs_4_, ...), custom_call_target="tpu_custom_call" | custom-call | flops 1000000000 | bytes 12582912 | tf_op jit(solution)/shard_map/main/pallas_call | solution.py:298
  129.8 0.0 collective-permute-done.refs_5_
  129.8 0.0 collective-permute-done.1.refs_6_
  129.8 6.3 %late.1 = f32[32,128,256]{2,1,0:T(8,128)} custom-call(s32[64]{0:T(128)S(1)} %copy-done.3, s32[64,16]{1,0:T(8,128)S(1)} %copy.10.refs_0_.refs_1_, s32[1]{0:T(128)S(6)} %copy.13.pivots_ref.refs_1_.refs_2_, f32[16,2,16,128]{3,2,1,0:T(8,128)S(1)} %bitcast.12, f32[16,2,48,128]{3,2,1,0:T(8,128)S(1)} %bitcast.9, ...), custom_call_target="tpu_custom_call", output_to_operand_aliasing={{}: (9, {})} | custom-call | flops 100000000 | bytes 4194304 | tf_op jit(solution)/shard_map/late/pallas_call | solution.py:312
Async XLA Ops:
  0.0 42.3 %copy-start.3 = (s32[64]{0:T(128)S(1)}, s32[64]{0:T(128)}, u32[]{:S(2)}) copy-start(s32[64]{0:T(128)} %refs_0_.5) | copy-start | bytes 772
  0.8 1.2 copy-start.2
  4.2 38.1 %all-to-all-start = ((f32[32,64,128]{2,1,0:T(8,128)}), f32[32,64,128]{2,1,0:T(8,128)S(1)}, u32[]{:S(2)}, u32[]{:S(2)}) async-start(f32[32,64,128]{2,1,0:T(8,128)} %bitcast), calls=%async_computation | async-start | bytes 2097152 | tf_op jit(solution)/shard_map/all_to_all | solution.py:250
  16.1 104.7 %collective-permute-start.6 = (f32[32,128,256]{2,1,0:T(8,128)}, f32[32,128,256]{2,1,0:T(8,128)}, u32[]{:S(2)}, u32[]{:S(2)}) collective-permute-start(f32[32,128,256]{2,1,0:T(8,128)} %bitcast.5), channel_id=1, source_target_pairs={{0,1},{2,3},{4,5},{6,7},{8,9},{10,11},{12,13},{14,15},{16,17},{18,... | collective-permute-start | bytes 12582920 | tf_op jit(solution)/shard_map/ppermute | solution.py:243
  60.4 21.9 %all-to-all-start.2 = ((f32[32,48,128]{2,1,0:T(8,128)}), f32[32,48,128]{2,1,0:T(8,128)S(1)}, u32[]{:S(2)}, u32[]{:S(2)}) async-start(f32[32,48,128]{2,1,0:T(8,128)} %get-tuple-element.14), calls=%async_computation.2 | async-start | bytes 1572864 | tf_op jit(solution)/shard_map/all_to_all | solution.py:261
  64.4 2.2 %copy-start = (f32[1,32,128,256]{3,2,1,0:T(8,128)S(1)}, f32[1,32,128,256]{3,2,1,0:T(8,128)}, u32[]{:S(2)}) copy-start(f32[1,32,128,256]{3,2,1,0:T(8,128)} %param.6) | copy-start | bytes 12582916
  67.8 16.7 %collective-permute-start.2 = (f32[128,256]{1,0:T(8,128)S(1)}, f32[128,256]{1,0:T(8,128)S(1)}, u32[]{:S(2)}, u32[]{:S(2)}) collective-permute-start(f32[128,256]{1,0:T(8,128)S(1)} %top.1.own_ref.refs_4_), channel_id=1, source_target_pairs={{0,2},{2,4},{4,6},{6,0},{1,3},{3,5},{5,7},{7,1},{8,10},{10,12},{12... | collective-permute-start | bytes 393224 | tf_op jit(solution)/shard_map/ppermute | solution.py:279
  69.1 15.4 %collective-permute-start.3 = (f32[128,256]{1,0:T(8,128)S(1)}, f32[128,256]{1,0:T(8,128)S(1)}, u32[]{:S(2)}, u32[]{:S(2)}) collective-permute-start(f32[128,256]{1,0:T(8,128)S(1)} %top.1.own_ref.refs_4_), channel_id=1, source_target_pairs={{0,4},{2,6},{4,0},{6,2},{1,5},{3,7},{5,1},{7,3},{8,12},{10,14},{12... | collective-permute-start | bytes 393224 | tf_op jit(solution)/shard_map/ppermute | solution.py:279
  71.7 12.8 %collective-permute-start.4 = (f32[128,256]{1,0:T(8,128)S(1)}, f32[128,256]{1,0:T(8,128)S(1)}, u32[]{:S(2)}, u32[]{:S(2)}) collective-permute-start(f32[128,256]{1,0:T(8,128)S(1)} %top.1.own_ref.refs_4_), channel_id=1, source_target_pairs={{0,6},{2,0},{4,2},{6,4},{1,7},{3,1},{5,3},{7,5},{8,14},{10,8},{12,... | collective-permute-start | bytes 393224 | tf_op jit(solution)/shard_map/ppermute | solution.py:279
  82.3 38.5 %copy-start.1 = (f32[1,32,128,256]{3,2,1,0:T(8,128)S(1)}, f32[1,32,128,256]{3,2,1,0:T(8,128)}, u32[]{:S(2)}) copy-start(f32[1,32,128,256]{3,2,1,0:T(8,128)} %param.6) | copy-start | bytes 12582916
  82.3 47.5 %collective-permute-start.1 = (f32[16,2,48,128]{3,2,1,0:T(8,128)S(1)}, f32[16,2,48,128]{3,2,1,0:T(8,128)S(1)}, u32[]{:S(2)}, u32[]{:S(2)}) collective-permute-start(f32[16,2,48,128]{3,2,1,0:T(8,128)S(1)} %bitcast.8), channel_id=1, source_target_pairs={{0,1},{2,3},{4,5},{6,7},{8,9},{10,11},{12,13},{14,15},{16,17},{18,... | collective-permute-start | bytes 2359304 | tf_op jit(solution)/shard_map/ppermute | solution.py:310
  112.1 8.7 %collective-permute-start.5 = (f32[384,256]{1,0:T(8,128)S(1)}, f32[384,256]{1,0:T(8,128)S(1)}, u32[]{:S(2)}, u32[]{:S(2)}) collective-permute-start(f32[384,256]{1,0:T(8,128)S(1)} %get-tuple-element.16), channel_id=1, source_target_pairs={{0,1},{2,3},{4,5},{6,7},{8,9},{10,11},{12,13},{14,15},{16,17},{18,... | collective-permute-start | bytes 1179656 | tf_op jit(solution)/shard_map/ppermute | solution.py:292
  113.4 16.4 %collective-permute-start = (f32[16,2,16,128]{3,2,1,0:T(8,128)S(1)}, f32[16,2,16,128]{3,2,1,0:T(8,128)S(1)}, u32[]{:S(2)}, u32[]{:S(2)}) collective-permute-start(f32[16,2,16,128]{3,2,1,0:T(8,128)S(1)} %bitcast.11), channel_id=1, source_target_pairs={{0,1},{2,3},{4,5},{6,7},{8,9},{10,11},{12,13},{14,15},{16,17},{18,... | collective-permute-start | bytes 786440 | tf_op jit(solution)/shard_map/ppermute | solution.py:293

commit v2 on v1

v2 whole, which is shorter than its diff:
```python
import jax
import jax.numpy as jnp
from jax import lax
from jax.experimental import pallas as pl
from jax.experimental.pallas import tpu as pltpu
from jax.sharding import PartitionSpec as P

F32 = jnp.float32
BLOCK = 128
WIDTH = 256
BASE = 64
GROUP = 16
CHUNK = 8
VMEM = pl.BlockSpec(memory_space=pltpu.VMEM)
HBM = pl.BlockSpec(memory_space=pltpu.HBM)
SMEM = pl.BlockSpec(memory_space=pltpu.SMEM)


def dot(a, b, ca=1, cb=0):
    return lax.dot_general(
        a, b, (((ca,), (cb,)), ((), ())),
        precision=lax.Precision.HIGHEST, preferred_element_type=F32,
    )


def split(a):
    high = a.astype(jnp.bfloat16)
    return high, (a - high.astype(F32)).astype(jnp.bfloat16)


def dot_split(a, b):
    def part(x, y):
        return lax.dot_general(x, y, (((1,), (0,)), ((), ())), preferred_element_type=F32)

    (ah, al), (bh, bl) = split(a), b
    return part(ah, bh) + (part(ah, bl) + part(al, bh))


def targets_of(maps_ref, child, row, rows):
    cycles = maps_ref.shape[1] // rows
    targets = [maps_ref[child, rows * i + row] // rows for i in range(cycles)]
    first = jnp.int32(0)
    found = jnp.int32(0)
    for i in range(cycles):
        hit = targets[i] == 0
        first = jnp.where(hit, i, first)
        found = jnp.where(hit, 1, found)
    return targets, first, found


def slot_block(slot, first):
    if slot == 0:
        return first
    return jnp.where(first >= slot, slot - 1, slot)


def pick(values, at):
    out = values[0]
    for i in range(1, len(values)):
        out = jnp.where(at == i, values[i], out)
    return out


def child_of(parents_ref, front, which):
    found = jnp.int32(0)
    for d in range(parents_ref.shape[0] // 2):
        found = jnp.where(parents_ref[2 * d + which] == front, 2 * d + which, found)
    return found


def spread_kernel(maps_ref, children_ref, out_ref, hold_ref, targets_ref, sem_maps, sem, *, rows):
    front, row = lax.axis_index("front"), lax.axis_index("row")
    maps = pltpu.make_async_copy(maps_ref, targets_ref, sem_maps)
    maps.start()
    copies = [
        pltpu.make_async_copy(children_ref.at[c], hold_ref.at[c], sem.at[c]) for c in range(2)
    ]
    for copy in copies:
        copy.start()
    cycles = children_ref.shape[1]
    maps.wait()
    for c in range(2):
        _, first, _ = targets_of(targets_ref, 2 * front + c, row, rows)
        copies[c].wait()
        for s in range(cycles):
            at = (c * cycles + s) * 8
            for half in range(2):
                tiles = hold_ref[c, slot_block(s, first), :, half * 128:(half + 1) * 128]
                out_ref[:, half, at:at + 8, :] = tiles.reshape(BLOCK // 8, 8, 128)


def route_kernel(parents_ref, in_ref, first_ref, rest_ref):
    fronts, depth = in_ref.shape[0], in_ref.shape[1]
    half = depth // 2
    for d in range(fronts):
        for c in range(2):
            to = parents_ref[2 * d + c]
            first_ref[to, c * 8:(c + 1) * 8, :] = in_ref[d, c * half:c * half + 8, :]
            rest_ref[to, c * (half - 8):(c + 1) * (half - 8), :] = in_ref[
                d, c * half + 8:(c + 1) * half, :
            ]


def tile_block(ref, at):
    return jnp.concatenate(
        [ref[:, half, at:at + 8, :].reshape(BLOCK, 128) for half in range(2)], axis=1
    )


def top_kernel(parents_ref, maps_ref, panel_ref, pieces_ref, out_ref, first_ref, *, rows):
    front, row = lax.axis_index("front"), lax.axis_index("row")
    total = panel_ref[...]
    for c in range(2):
        first_ref[c] = tile_block(pieces_ref, c * 8)
        child = child_of(parents_ref, front, c)
        total += first_ref[c] * targets_of(maps_ref, child, row, rows)[2].astype(F32)
    out_ref[...] = total


def invert_base(a):
    n = a.shape[0]
    r = lax.broadcasted_iota(jnp.int32, (n, n), 0)
    l = lax.broadcasted_iota(jnp.int32, (n, n), 1)
    both = jnp.concatenate([a, jnp.where(r == l, 1.0, 0.0).astype(F32)], axis=1)
    done = []
    for g in range(0, n, GROUP):
        below = n - g
        sub = lax.broadcasted_iota(jnp.int32, (below, 2 * n), 0)
        columns = [
            jnp.broadcast_to(both[:, g + q:g + q + 1], (below, 2 * n)) for q in range(GROUP)
        ]
        diag = jnp.ones((GROUP, 2 * n), F32)
        for q in range(GROUP):
            column = columns[q]
            pivot = column[q:q + 1, :]
            diag = jnp.where(sub[:GROUP] == q, pivot, diag)
            f = jnp.where(sub > q, column, 0.0) * (1.0 / pivot)
            for k in range(q + 1, GROUP):
                columns[k] = columns[k] - f * columns[k][q:q + 1, :]
            both = both - f * both[q:q + 1, :]
        done.append(both[:GROUP] * lax.rsqrt(diag))
        both = both[GROUP:]
    return jnp.concatenate(done, axis=0)[:, n:]


def invert_factor(a):
    n = a.shape[0]
    if n == BASE:
        return invert_base(a)
    h = n // 2
    w1 = invert_factor(a[:h, :h])
    l21 = dot(a[h:, :h], w1, 1, 1)
    w2 = invert_factor(a[h:, h:] - dot(l21, l21, 1, 1))
    w21 = -dot(w2, dot(l21, w1))
    return jnp.concatenate(
        [
            jnp.concatenate([w1, jnp.zeros((h, h), F32)], axis=1),
            jnp.concatenate([w21, w2], axis=1),
        ],
        axis=0,
    )


def factor_kernel(pivots_ref, own_ref, r1_ref, r2_ref, r3_ref, solve_ref, send_ref, all_ref):
    row = lax.axis_index("row")
    for s, ref in enumerate((own_ref, r1_ref, r2_ref, r3_ref)):
        at = pl.multiple_of(lax.rem(row + 4 - s, 4) * BLOCK, BLOCK)
        all_ref[pl.ds(at, BLOCK), :] = ref[...]
    pivots = pivots_ref[0]
    r = lax.broadcasted_iota(jnp.int32, (WIDTH, WIDTH), 0)
    l = lax.broadcasted_iota(jnp.int32, (WIDTH, WIDTH), 1)
    both = (r < pivots) & (l < pivots)
    diag = all_ref[0:WIDTH, :]
    low = jnp.where(r >= l, diag, 0.0)
    strict = jnp.where(r > l, diag, 0.0)
    mirrored = low + strict.T
    masked = jnp.where(both, mirrored, jnp.where(r == l, 1.0, 0.0))
    inverse = jnp.where(both, invert_factor(masked), 0.0)
    solved = dot(all_ref[...], inverse, 1, 1)
    top = jnp.where(r >= l, solved[:WIDTH], 0.0)
    solve_t = inverse - jnp.where(r < pivots, 0.0, dot(top, inverse))
    update_t = dot(solved[WIDTH:], inverse)
    solve_ref[...] = solve_t.T
    send_ref[0:WIDTH, :] = update_t.T
    send_ref[WIDTH:, :] = own_ref[...]


def finish_kernel(parents_ref, maps_ref, orders_ref, pivots_ref, top_ref, solve_ref, sent_ref,
                  first_ref, rest_ref, lfirst_ref, lrest_ref, panel_ref, left_ref, out_ref,
                  hold_ref, x_ref, sem_hold, sem_x, sem_out, *, rows):
    front, row, col = lax.axis_index("front"), lax.axis_index("row"), lax.axis_index("col")
    cycles = panel_ref.shape[0]
    child_cycles = maps_ref.shape[1] // rows
    orders, pivots = orders_ref[0], pivots_ref[0]
    chunks = [pl.ds(k, CHUNK) for k in range(0, cycles, CHUNK)]
    hold = [
        pltpu.make_async_copy(panel_ref.at[at], hold_ref.at[at], sem_hold.at[k])
        for k, at in enumerate(chunks)
    ]
    store = [
        pltpu.make_async_copy(hold_ref.at[at], out_ref.at[at], sem_out.at[k])
        for k, at in enumerate(chunks)
    ]
    for k, at in enumerate(chunks):
        hold[k].start()

        @pl.when(col == 0)
        def _():
            pltpu.make_async_copy(panel_ref.at[at], x_ref.at[at], sem_x.at[k]).start()

        @pl.when(col != 0)
        def _():
            pltpu.make_async_copy(left_ref.at[at], x_ref.at[at], sem_x.at[k]).start()

    places = []
    for c in range(2):
        targets, first, _ = targets_of(maps_ref, child_of(parents_ref, front, c), row, rows)
        for s in range(child_cycles):
            places.append((pick(targets, slot_block(s, first)), c, s))

    def child_block(first, rest, c, s):
        if s == 0:
            return first[c]
        return tile_block(rest, (c * (child_cycles - 1) + s - 1) * 8)

    lane = lax.broadcasted_iota(jnp.int32, (1, WIDTH), 1)
    scale = jnp.where((col != 0) | (lane >= pivots), 1.0, 0.0)
    right = split(jnp.where(col == 0, solve_ref[...], -sent_ref[0:WIDTH, :]))
    for k, at in enumerate(chunks):
        hold[k].wait()
        pltpu.make_async_copy(panel_ref.at[at], x_ref.at[at], sem_x.at[k]).wait()
        if k == 0:
            hold_ref[0] = top_ref[...]
            x_ref[0] = jnp.where(col == 0, top_ref[...], sent_ref[WIDTH:, :])
        for place, c, s in places:
            @pl.when((place != 0) & (place // CHUNK == k))
            def _():
                hold_ref[place] += child_block(first_ref, rest_ref, c, s)

                @pl.when(col == 0)
                def _():
                    x_ref[place] += child_block(first_ref, rest_ref, c, s)

                @pl.when(col != 0)
                def _():
                    x_ref[place] += child_block(lfirst_ref, lrest_ref, c, s)

        y = dot_split(x_ref[at].reshape(CHUNK * BLOCK, WIDTH), right)
        for i in range(CHUNK):
            cycle = k * CHUNK + i
            start = (cycle * rows + row) * BLOCK
            z = hold_ref[cycle] * scale + y[i * BLOCK:(i + 1) * BLOCK]
            keep = start < orders
            if cycle == 0:
                g = row * BLOCK + lax.broadcasted_iota(jnp.int32, (BLOCK, WIDTH), 0)
                j = col * WIDTH + lax.broadcasted_iota(jnp.int32, (BLOCK, WIDTH), 1)
                keep = keep & (g >= j)
            hold_ref[cycle] = jnp.where(keep, z, 0.0)
        store[k].start()
    for copy in store:
        copy.wait()


def on_device(panel, children, parents, row_maps, orders, pivots):
    rows = lax.axis_size("row")
    fronts = lax.axis_size("front")
    cycles = panel.shape[1]
    child_cycles = children.shape[1]
    panel = panel[0]
    depth = 2 * (child_cycles - 1) * 8
    pieces = (BLOCK // 8, 2)
    params = pltpu.CompilerParams(vmem_limit_bytes=32 * 2**20)
    shape = lambda *dims: jax.ShapeDtypeStruct(dims, F32)
    to_right = [(0, 1)]

    def exchange(value):
        return lax.all_to_all(value.reshape(fronts, -1, 128), "front", 0, 0, tiled=True)

    spread = pl.pallas_call(
        lambda *refs: spread_kernel(*refs, rows=rows),
        out_shape=shape(*pieces, depth + 16, 128),
        in_specs=[HBM, HBM], out_specs=VMEM,
        scratch_shapes=[
            pltpu.VMEM(children.shape, F32), pltpu.SMEM(row_maps.shape, jnp.int32),
            pltpu.SemaphoreType.DMA, pltpu.SemaphoreType.DMA((2,)),
        ],
        compiler_params=pltpu.CompilerParams(vmem_limit_bytes=62 * 2**20), name="spread",
    )(row_maps, children)
    spread = exchange(spread)
    first, rest = pl.pallas_call(
        route_kernel, out_shape=(shape(fronts, 16, 128), shape(fronts, depth, 128)),
        in_specs=[SMEM, VMEM], out_specs=(VMEM, VMEM), compiler_params=params, name="route",
    )(parents, spread)
    first, panel = lax.optimization_barrier((first, panel))
    left = lax.ppermute(panel, "col", to_right)
    first = exchange(first)
    panel_top = panel[0]
    top, first = pl.pallas_call(
        lambda *refs: top_kernel(*refs, rows=rows),
        out_shape=(shape(BLOCK, WIDTH), shape(2, BLOCK, WIDTH)),
        in_specs=[SMEM, SMEM, VMEM, VMEM], out_specs=(VMEM, VMEM),
        compiler_params=params, name="top",
    )(parents, row_maps, panel_top, first.reshape(*pieces, 16, 128))
    rest, top = lax.optimization_barrier((rest, top))
    rest = exchange(rest).reshape(*pieces, depth, 128)
    others = [
        lax.ppermute(top, "row", [(i, (i + s) % rows) for i in range(rows)]) for s in (1, 2, 3)
    ]
    left_first = lax.ppermute(first, "col", to_right)
    *others, left_first = lax.optimization_barrier((*others, left_first))
    solve, send = pl.pallas_call(
        factor_kernel,
        out_shape=(shape(WIDTH, WIDTH), shape(WIDTH + BLOCK, WIDTH)),
        in_specs=[SMEM, VMEM, VMEM, VMEM, VMEM], out_specs=(VMEM, VMEM),
        scratch_shapes=[pltpu.VMEM((4 * BLOCK, WIDTH), F32)],
        compiler_params=params, name="factor",
        cost_estimate=pl.CostEstimate(flops=2 * 10**9, bytes_accessed=2**21, transcendentals=0),
    )(pivots, top, *others)
    sent = lax.ppermute(send, "col", to_right)

    rest, solve = lax.optimization_barrier((rest, solve))
    left_rest = lax.ppermute(rest, "col", to_right)
    steps = cycles // CHUNK
    out = pl.pallas_call(
        lambda *refs: finish_kernel(*refs, rows=rows),
        out_shape=shape(*panel.shape),
        in_specs=[SMEM] * 4 + [VMEM] * 7 + [HBM] * 2, out_specs=HBM,
        scratch_shapes=[pltpu.VMEM(panel.shape, F32)] * 2 + [pltpu.SemaphoreType.DMA((steps,))] * 3,
        compiler_params=pltpu.CompilerParams(vmem_limit_bytes=57 * 2**20), name="finish",
        cost_estimate=pl.CostEstimate(flops=10**9, bytes_accessed=12 * 2**20, transcendentals=0),
    )(
        parents, row_maps, orders, pivots, top, solve, sent,
        first, rest, left_first, left_rest, panel, left,
    )
    return out[None]


def solution(mesh):
    in_specs = (
        P("front", None, "row", "col"),
        P("front", None, "row", "col"),
        P(),
        P(),
        P("front"),
        P("front"),
    )
    out_specs = P("front", None, "row", "col")
    return jax.shard_map(
        on_device, mesh=mesh, in_specs=in_specs, out_specs=out_specs, check_vma=False
    )
```

time: 137 us -> 110 us (0.80)
  Pallas kernels: 47.8 us -> 24.7 us
  blocking collectives: 16.5 us -> 38.1 us
  waiting for transfers between devices: 39.6 us -> 21.4 us
  starting transfers between devices: 26.5 us -> 19.5 us
    all_to_all x2, waiting for transfers between devices: 34.4 us -> 9.49 us  [exchange(): lax.all_to_all(value.reshape(fronts, -1, 128), 'front', 0, 0, tiled=True)]
    pallas_call x6 -> x5, Pallas kernels: 47.8 us -> 24.7 us  [the longest x1 10.3 us: on_device(): pl.pallas_call(factor_kernel, out_shape=(shape(WIDTH, WIDTH), shape(WIDTH...]
    all_to_all x1, blocking collectives: 16.5 us -> 38.1 us  [exchange(): lax.all_to_all(value.reshape(fronts, -1, 128), 'front', 0, 0, tiled=True)]
    all_to_all x2, starting transfers between devices: 15.8 us -> 10.3 us  [exchange(): lax.all_to_all(value.reshape(fronts, -1, 128), 'front', 0, 0, tiled=True)]
    ppermute x3, waiting for transfers between devices: 0.01 us -> 5.17 us  [on_device(): lax.ppermute(top, 'row', [(i, (i + s) % rows) for i in range(rows)])]
    ppermute x1, waiting for transfers between devices: 5.25 us -> 6.74 us  [on_device(): sent = lax.ppermute(send, 'col', to_right)]
    unnamed x9 -> x19, local copies, waits for them, and re-layouts: 4.21 us -> 3.14 us
  transfers between devices with their start and end apart: 9 -> 9, of which waited for: 3 -> 5; matrix products, arithmetic and copies ran while one was open for 0% -> 1% of each run, Pallas kernels for 29% -> 11%
where the time goes in v2:
time: 110 us; the launch traced here: 109 us
  blocking collectives  38.1 us (35%)
  Pallas kernels  24.7 us (22%)
  waiting for transfers between devices  21.4 us (19%)
  starting transfers between devices  19.5 us (18%)
  local copies, waits for them, and re-layouts  4.06 us (4%)
  between operations  1.61 us (1%)
    all_to_all x1, blocking collectives, exchange(): lax.all_to_all(value.reshape(fronts, -1, 128), 'front', 0, 0, tiled=True)  38.1 us
    pallas_call x1, Pallas kernels, on_device(): pl.pallas_call(factor_kernel, out_shape=(shape(WIDTH, WIDTH), shape(WIDTH...  10.3 us
    all_to_all x2, starting transfers between devices, exchange(): lax.all_to_all(value.reshape(fronts, -1, 128), 'front', 0, 0, tiled=True)  10.3 us
    all_to_all x2, waiting for transfers between devices, exchange(): lax.all_to_all(value.reshape(fronts, -1, 128), 'front', 0, 0, tiled=True)  9.49 us
    pallas_call x1, Pallas kernels, on_device(): pl.pallas_call(lambda *refs: finish_kernel(*refs, rows=rows), out_shape=s...  9.11 us
    ppermute x1, waiting for transfers between devices, on_device(): sent = lax.ppermute(send, 'col', to_right)  6.74 us
    ppermute x3, waiting for transfers between devices, on_device(): lax.ppermute(top, 'row', [(i, (i + s) % rows) for i in range(rows)])  5.17 us
    ppermute x3, starting transfers between devices, on_device(): lax.ppermute(top, 'row', [(i, (i + s) % rows) for i in range(rows)])  3.85 us
  transfers between devices with their start and end apart: 9, of which 5 were waited for; matrix products, arithmetic and copies ran while one was open for 1% of the time, Pallas kernels for 11%

profile of v2, /device:TPU:1, one launch (start us, length us, event | category | flops | bytes accessed | tf_op | source)
XLA Modules:
  0.0 109.4 jit_solution(16453671233170447538)
XLA Ops:
  0.0 0.0 copy-start.4
  0.0 1.4 %copy.9.refs_0_.refs_1_ = s32[64,16]{1,0:T(8,128)} copy(s32[64,16]{0,1:T(8,128)} %param.9) | data formatting | bytes 8192 | tf_op args[3]
  1.4 0.0 copy-start
  1.4 2.5 %spread.1 = f32[16,2,64,128]{3,2,1,0:T(8,128)} custom-call(s32[64,16]{1,0:T(8,128)} %copy.9.refs_0_.refs_1_, f32[2,4,128,256]{3,2,1,0:T(8,128)} %refs_1_.3), custom_call_target="tpu_custom_call" | custom-call | tf_op jit(solution)/shard_map/spread/pallas_call | solution.py:279
  3.9 38.1 %all_to_all.15.in_ref = f32[32,64,128]{2,1,0:T(8,128)S(1)} all-to-all(f32[32,64,128]{2,1,0:T(8,128)} %bitcast.11), channel_id=1, replica_groups=mesh['front'=32,'row'=4,'col'=2] {'front'}, dimensions={0} | all-to-all | bytes 2097152 | tf_op jit(solution)/shard_map/all_to_all | solution.py:277
  42.0 0.0 copy-done.4
  42.0 1.6 %route.1 = (f32[32,16,128]{2,1,0:T(8,128)}, f32[32,48,128]{2,1,0:T(8,128)}) custom-call(s32[64]{0:T(128)S(1)} %copy-done.4, f32[32,64,128]{2,1,0:T(8,128)S(1)} %all_to_all.15.in_ref), custom_call_target="tpu_custom_call" | custom-call | tf_op jit(solution)/shard_map/route/pallas_call | solution.py:290
  43.6 1.3 %collective-permute-start.6 = (f32[32,128,256]{2,1,0:T(8,128)}, f32[32,128,256]{2,1,0:T(8,128)}, u32[]{:S(2)}, u32[]{:S(2)}) collective-permute-start(f32[32,128,256]{2,1,0:T(8,128)} %bitcast.8), channel_id=1, source_target_pairs={{0,1},{2,3},{4,5},{6,7},{8,9},{10,11},{12,13},{14,15},{16,17},{18,... | collective-permute-start | bytes 12582920 | tf_op jit(solution)/shard_map/ppermute | solution.py:295
  44.9 6.4 %all-to-all-start.1 = ((f32[32,16,128]{2,1,0:T(8,128)}), f32[32,16,128]{2,1,0:T(8,128)S(1)}, u32[]{:S(2)}, u32[]{:S(2)}) async-start(f32[32,16,128]{2,1,0:T(8,128)} %get-tuple-element.24), calls=%async_computation.1 | async-start | bytes 524288 | tf_op jit(solution)/shard_map/all_to_all | solution.py:277
  51.2 0.9 slice_bitcast_fusion.refs_2_
  52.2 9.5 %all-to-all-done.1 = f32[32,16,128]{2,1,0:T(8,128)S(1)} async-done(((f32[32,16,128]{2,1,0:T(8,128)}), f32[32,16,128]{2,1,0:T(8,128)S(1)}, u32[]{:S(2)}, u32[]{:S(2)}) %all-to-all-start.1) | async-done | bytes 262176 | tf_op jit(solution)/shard_map/all_to_all | solution.py:277
  61.6 0.0 copy-done
  61.6 1.2 %top.1 = (f32[128,256]{1,0:T(8,128)S(1)}, f32[2,128,256]{2,1,0:T(8,128)S(1)}) custom-call(s32[64]{0:T(128)S(1)} %copy-done.4, s32[64,16]{1,0:T(8,128)S(1)} %copy-done, f32[128,256]{1,0:T(8,128)S(1)} %slice_bitcast_fusion.refs_2_, f32[16,2,16,128]{3,2,1,0:T(8,128)S(1)} %bitcast.7), custom_call_target="tpu_custom_call" | custom-call | tf_op jit(solution)/shard_map/top/pallas_call | solution.py:298
  62.9 0.0 copy-start.1
  62.9 0.0 copy-start.3
  62.9 3.9 %all-to-all-start.2 = ((f32[32,48,128]{2,1,0:T(8,128)}), f32[32,48,128]{2,1,0:T(8,128)S(1)}, u32[]{:S(2)}, u32[]{:S(2)}) async-start(f32[32,48,128]{2,1,0:T(8,128)} %get-tuple-element.27), calls=%async_computation.2 | async-start | bytes 1572864 | tf_op jit(solution)/shard_map/all_to_all | solution.py:277
  66.8 1.3 %collective-permute-start.3 = (f32[2,128,256]{2,1,0:T(8,128)S(1)}, f32[2,128,256]{2,1,0:T(8,128)S(1)}, u32[]{:S(2)}, u32[]{:S(2)}) collective-permute-start(f32[2,128,256]{2,1,0:T(8,128)S(1)} %get-tuple-element.28.refs_7_), channel_id=1, source_target_pairs={{0,1},{2,3},{4,5},{6,7},{8,9},{10,11},{12,13},{14,15},{16,17},{18,... | collective-permute-start | bytes 786440 | tf_op jit(solution)/shard_map/ppermute | solution.py:309
  68.1 2.8 %collective-permute-start.2 = (f32[128,256]{1,0:T(8,128)S(1)}, f32[128,256]{1,0:T(8,128)S(1)}, u32[]{:S(2)}, u32[]{:S(2)}) collective-permute-start(f32[128,256]{1,0:T(8,128)S(1)} %get-tuple-element.26.own_ref.refs_4_), channel_id=1, source_target_pairs={{0,6},{2,0},{4,2},{6,4},{1,7},{3,1},{5,3},{7,5},{8,14},{10,8},{12,... | collective-permute-start | bytes 393224 | tf_op jit(solution)/shard_map/ppermute | solution.py:307
  70.9 0.3 collective-permute-start.1
  71.3 0.7 collective-permute-start
  72.6 1.6 %collective-permute-done.2.r3_ref = f32[128,256]{1,0:T(8,128)S(1)} collective-permute-done((f32[128,256]{1,0:T(8,128)S(1)}, f32[128,256]{1,0:T(8,128)S(1)}, u32[]{:S(2)}, u32[]{:S(2)}) %collective-permute-start.2) | collective-permute-done | bytes 131104 | tf_op jit(solution)/shard_map/ppermute | solution.py:307
  74.2 2.1 %collective-permute-done.1.r2_ref = f32[128,256]{1,0:T(8,128)S(1)} collective-permute-done((f32[128,256]{1,0:T(8,128)S(1)}, f32[128,256]{1,0:T(8,128)S(1)}, u32[]{:S(2)}, u32[]{:S(2)}) %collective-permute-start.1) | collective-permute-done | bytes 131104 | tf_op jit(solution)/shard_map/ppermute | solution.py:307
  76.3 1.4 %collective-permute-done.r1_ref = f32[128,256]{1,0:T(8,128)S(1)} collective-permute-done((f32[128,256]{1,0:T(8,128)S(1)}, f32[128,256]{1,0:T(8,128)S(1)}, u32[]{:S(2)}, u32[]{:S(2)}) %collective-permute-start) | collective-permute-done | bytes 131104 | tf_op jit(solution)/shard_map/ppermute | solution.py:307
  77.8 0.0 collective-permute-done.3.refs_9_
  77.8 0.0 copy-start.8
  77.8 10.3 %factor.1 = (f32[256,256]{1,0:T(8,128)S(1)}, f32[384,256]{1,0:T(8,128)S(1)}) custom-call(s32[1]{0:T(128)S(6)} %copy.11.pivots_ref.refs_3_, f32[128,256]{1,0:T(8,128)S(1)} %get-tuple-element.26.own_ref.refs_4_, f32[128,256]{1,0:T(8,128)S(1)} %collective-permute-done.r1_ref, f32[128,256]{1,0:T(8,128)S(1)} %collective-permute-done.1.r2_ref, ...), custom_call_target="tpu_custom_call" | custom-call | flops 2000000000 | bytes 2097152 | tf_op jit(solution)/shard_map/factor/pallas_call | solution.py:311
  88.1 0.0 copy-done.1
  88.2 0.0 copy-done.3
  88.2 0.0 copy-start.2
  88.2 0.7 copy-done.2
  88.9 0.0 all-to-all-done.2
  88.9 0.0 copy-start.5
  88.9 1.3 %collective-permute-start.5 = (f32[16,2,48,128]{3,2,1,0:T(8,128)S(1)}, f32[16,2,48,128]{3,2,1,0:T(8,128)S(1)}, u32[]{:S(2)}, u32[]{:S(2)}) collective-permute-start(f32[16,2,48,128]{3,2,1,0:T(8,128)S(1)} %bitcast.12), channel_id=1, source_target_pairs={{0,1},{2,3},{4,5},{6,7},{8,9},{10,11},{12,13},{14,15},{16,17},{18,... | collective-permute-start | bytes 2359304 | tf_op jit(solution)/shard_map/ppermute | solution.py:322
  90.2 1.5 %collective-permute-start.4 = (f32[384,256]{1,0:T(8,128)S(1)}, f32[384,256]{1,0:T(8,128)S(1)}, u32[]{:S(2)}, u32[]{:S(2)}) collective-permute-start(f32[384,256]{1,0:T(8,128)S(1)} %get-tuple-element.34), channel_id=1, source_target_pairs={{0,1},{2,3},{4,5},{6,7},{8,9},{10,11},{12,13},{14,15},{16,17},{18,... | collective-permute-start | bytes 1179656 | tf_op jit(solution)/shard_map/ppermute | solution.py:319
  92.3 6.7 %collective-permute-done.4.refs_6_ = f32[384,256]{1,0:T(8,128)S(1)} collective-permute-done((f32[384,256]{1,0:T(8,128)S(1)}, f32[384,256]{1,0:T(8,128)S(1)}, u32[]{:S(2)}, u32[]{:S(2)}) %collective-permute-start.4) | collective-permute-done | bytes 393248 | tf_op jit(solution)/shard_map/ppermute | solution.py:319
  99.0 0.0 copy-start.7
  99.0 0.0 collective-permute-done.5.refs_10_
  99.0 0.0 copy-start.6
  99.0 0.0 collective-permute-done.6.refs_12_
  99.0 0.0 copy-done.8
  99.0 0.0 copy-done.5
  99.1 0.7 copy-done.7
  99.8 0.3 copy-done.6
  100.1 9.1 %finish.1 = f32[32,128,256]{2,1,0:T(8,128)} custom-call(s32[64]{0:T(128)} %refs_0_.4, s32[64,16]{1,0:T(8,128)} %copy.9.refs_0_.refs_1_, s32[1]{0:T(128)S(6)} %copy.10.refs_2_, s32[1]{0:T(128)S(6)} %copy.11.pivots_ref.refs_3_, f32[128,256]{1,0:T(8,128)} %copy-done.3, f32[256,256]{1,0:T(8,128)} %copy-done.2, f32[384,256]{1,0:T(8,128)} %copy-done.7, ...), custom_call_target="tpu_custom_call" | custom-call | flops 1000000000 | bytes 12582912 | tf_op jit(solution)/shard_map/finish/pallas_call | solution.py:324
Async XLA Ops:
  0.0 42.0 %copy-start.4 = (s32[64]{0:T(128)S(1)}, s32[64]{0:T(128)}, u32[]{:S(2)}) copy-start(s32[64]{0:T(128)} %refs_0_.4) | copy-start | bytes 772
  1.4 60.2 %copy-start = (s32[64,16]{1,0:T(8,128)S(1)}, s32[64,16]{1,0:T(8,128)}, u32[]{:S(2)}) copy-start(s32[64,16]{1,0:T(8,128)} %copy.9.refs_0_.refs_1_) | copy-start | bytes 12292
  43.6 55.5 %collective-permute-start.6 = (f32[32,128,256]{2,1,0:T(8,128)}, f32[32,128,256]{2,1,0:T(8,128)}, u32[]{:S(2)}, u32[]{:S(2)}) collective-permute-start(f32[32,128,256]{2,1,0:T(8,128)} %bitcast.8), channel_id=1, source_target_pairs={{0,1},{2,3},{4,5},{6,7},{8,9},{10,11},{12,13},{14,15},{16,17},{18,... | collective-permute-start | bytes 12582920 | tf_op jit(solution)/shard_map/ppermute | solution.py:295
  44.9 16.8 %all-to-all-start.1 = ((f32[32,16,128]{2,1,0:T(8,128)}), f32[32,16,128]{2,1,0:T(8,128)S(1)}, u32[]{:S(2)}, u32[]{:S(2)}) async-start(f32[32,16,128]{2,1,0:T(8,128)} %get-tuple-element.24), calls=%async_computation.1 | async-start | bytes 524288 | tf_op jit(solution)/shard_map/all_to_all | solution.py:277
  62.9 25.3 %copy-start.1 = (f32[2,128,256]{2,1,0:T(8,128)}, f32[2,128,256]{2,1,0:T(8,128)S(1)}, u32[]{:S(2)}) copy-start(f32[2,128,256]{2,1,0:T(8,128)S(1)} %get-tuple-element.28.refs_7_) | copy-start | bytes 786436
  62.9 25.3 %copy-start.3 = (f32[128,256]{1,0:T(8,128)}, f32[128,256]{1,0:T(8,128)S(1)}, u32[]{:S(2)}) copy-start(f32[128,256]{1,0:T(8,128)S(1)} %get-tuple-element.26.own_ref.refs_4_) | copy-start | bytes 393220
  62.9 26.0 %all-to-all-start.2 = ((f32[32,48,128]{2,1,0:T(8,128)}), f32[32,48,128]{2,1,0:T(8,128)S(1)}, u32[]{:S(2)}, u32[]{:S(2)}) async-start(f32[32,48,128]{2,1,0:T(8,128)} %get-tuple-element.27), calls=%async_computation.2 | async-start | bytes 1572864 | tf_op jit(solution)/shard_map/all_to_all | solution.py:277
  66.8 11.0 %collective-permute-start.3 = (f32[2,128,256]{2,1,0:T(8,128)S(1)}, f32[2,128,256]{2,1,0:T(8,128)S(1)}, u32[]{:S(2)}, u32[]{:S(2)}) collective-permute-start(f32[2,128,256]{2,1,0:T(8,128)S(1)} %get-tuple-element.28.refs_7_), channel_id=1, source_target_pairs={{0,1},{2,3},{4,5},{6,7},{8,9},{10,11},{12,13},{14,15},{16,17},{18,... | collective-permute-start | bytes 786440 | tf_op jit(solution)/shard_map/ppermute | solution.py:309
  68.1 6.1 %collective-permute-start.2 = (f32[128,256]{1,0:T(8,128)S(1)}, f32[128,256]{1,0:T(8,128)S(1)}, u32[]{:S(2)}, u32[]{:S(2)}) collective-permute-start(f32[128,256]{1,0:T(8,128)S(1)} %get-tuple-element.26.own_ref.refs_4_), channel_id=1, source_target_pairs={{0,6},{2,0},{4,2},{6,4},{1,7},{3,1},{5,3},{7,5},{8,14},{10,8},{12,... | collective-permute-start | bytes 393224 | tf_op jit(solution)/shard_map/ppermute | solution.py:307
  70.9 5.4 %collective-permute-start.1 = (f32[128,256]{1,0:T(8,128)S(1)}, f32[128,256]{1,0:T(8,128)S(1)}, u32[]{:S(2)}, u32[]{:S(2)}) collective-permute-start(f32[128,256]{1,0:T(8,128)S(1)} %get-tuple-element.26.own_ref.refs_4_), channel_id=1, source_target_pairs={{0,4},{2,6},{4,0},{6,2},{1,5},{3,7},{5,1},{7,3},{8,12},{10,14},{12... | collective-permute-start | bytes 393224 | tf_op jit(solution)/shard_map/ppermute | solution.py:307
  71.3 6.5 %collective-permute-start = (f32[128,256]{1,0:T(8,128)S(1)}, f32[128,256]{1,0:T(8,128)S(1)}, u32[]{:S(2)}, u32[]{:S(2)}) collective-permute-start(f32[128,256]{1,0:T(8,128)S(1)} %get-tuple-element.26.own_ref.refs_4_), channel_id=1, source_target_pairs={{0,2},{2,4},{4,6},{6,0},{1,3},{3,5},{5,7},{7,1},{8,10},{10,12},{12... | collective-permute-start | bytes 393224 | tf_op jit(solution)/shard_map/ppermute | solution.py:307
  77.8 21.3 %copy-start.8 = (f32[2,128,256]{2,1,0:T(8,128)}, f32[2,128,256]{2,1,0:T(8,128)S(1)}, u32[]{:S(2)}) copy-start(f32[2,128,256]{2,1,0:T(8,128)S(1)} %collective-permute-done.3.refs_9_) | copy-start | bytes 786436
  88.2 0.7 copy-start.2
  88.9 10.2 %copy-start.5 = (f32[32,48,128]{2,1,0:T(8,128)}, f32[32,48,128]{2,1,0:T(8,128)S(1)}, u32[]{:S(2)}) copy-start(f32[32,48,128]{2,1,0:T(8,128)S(1)} %all-to-all-done.2) | copy-start | bytes 2359300
  88.9 10.2 %collective-permute-start.5 = (f32[16,2,48,128]{3,2,1,0:T(8,128)S(1)}, f32[16,2,48,128]{3,2,1,0:T(8,128)S(1)}, u32[]{:S(2)}, u32[]{:S(2)}) collective-permute-start(f32[16,2,48,128]{3,2,1,0:T(8,128)S(1)} %bitcast.12), channel_id=1, source_target_pairs={{0,1},{2,3},{4,5},{6,7},{8,9},{10,11},{12,13},{14,15},{16,17},{18,... | collective-permute-start | bytes 2359304 | tf_op jit(solution)/shard_map/ppermute | solution.py:322
  90.2 8.9 %collective-permute-start.4 = (f32[384,256]{1,0:T(8,128)S(1)}, f32[384,256]{1,0:T(8,128)S(1)}, u32[]{:S(2)}, u32[]{:S(2)}) collective-permute-start(f32[384,256]{1,0:T(8,128)S(1)} %get-tuple-element.34), channel_id=1, source_target_pairs={{0,1},{2,3},{4,5},{6,7},{8,9},{10,11},{12,13},{14,15},{16,17},{18,... | collective-permute-start | bytes 1179656 | tf_op jit(solution)/shard_map/ppermute | solution.py:319
  99.0 0.8 copy-start.7
  99.0 1.1 copy-start.6

commit v3 on v2

--- a/solution.py
+++ b/solution.py
@@ -68,37 +68,43 @@
     return found
 
 
-def spread_kernel(maps_ref, children_ref, out_ref, hold_ref, targets_ref, sem_maps, sem, *, rows):
-    front, row = lax.axis_index("front"), lax.axis_index("row")
-    maps = pltpu.make_async_copy(maps_ref, targets_ref, sem_maps)
-    maps.start()
+def spread_kernel(children_ref, out_ref, hold_ref, sem):
+    cycles = children_ref.shape[1]
+    blocks = [(c, i) for c in range(2) for i in range(cycles)]
     copies = [
-        pltpu.make_async_copy(children_ref.at[c], hold_ref.at[c], sem.at[c]) for c in range(2)
+        pltpu.make_async_copy(children_ref.at[c, i], hold_ref.at[c, i], sem.at[c, i])
+        for c, i in blocks
     ]
     for copy in copies:
         copy.start()
-    cycles = children_ref.shape[1]
-    maps.wait()
-    for c in range(2):
-        _, first, _ = targets_of(targets_ref, 2 * front + c, row, rows)
-        copies[c].wait()
-        for s in range(cycles):
-            at = (c * cycles + s) * 8
-            for half in range(2):
-                tiles = hold_ref[c, slot_block(s, first), :, half * 128:(half + 1) * 128]
-                out_ref[:, half, at:at + 8, :] = tiles.reshape(BLOCK // 8, 8, 128)
-
-
-def route_kernel(parents_ref, in_ref, first_ref, rest_ref):
+    for n, (c, i) in enumerate(blocks):
+        copies[n].wait()
+        for half in range(2):
+            tiles = hold_ref[c, i, :, half * 128:(half + 1) * 128]
+            out_ref[:, half, n * 8:(n + 1) * 8, :] = tiles.reshape(BLOCK // 8, 8, 128)
+
+
+def plan_kernel(maps_ref, out_ref, *, rows):
+    row = lax.axis_index("row")
+    for c in range(maps_ref.shape[0]):
+        out_ref[c] = targets_of(maps_ref, c, row, rows)[1]
+
+
+def route_kernel(parents_ref, plan_ref, in_ref, first_ref, rest_ref):
     fronts, depth = in_ref.shape[0], in_ref.shape[1]
-    half = depth // 2
+    cycles = depth // 16
     for d in range(fronts):
         for c in range(2):
             to = parents_ref[2 * d + c]
-            first_ref[to, c * 8:(c + 1) * 8, :] = in_ref[d, c * half:c * half + 8, :]
-            rest_ref[to, c * (half - 8):(c + 1) * (half - 8), :] = in_ref[
-                d, c * half + 8:(c + 1) * half, :
-            ]
+            first = plan_ref[2 * d + c]
+            for s in range(cycles):
+                at = pl.multiple_of((c * cycles + slot_block(s, first)) * 8, 8)
+                tile = in_ref[d, pl.ds(at, 8), :]
+                if s == 0:
+                    first_ref[to, c * 8:(c + 1) * 8, :] = tile
+                else:
+                    put = (c * (cycles - 1) + s - 1) * 8
+                    rest_ref[to, put:put + 8, :] = tile
 
 
 def tile_block(ref, at):
@@ -161,7 +167,7 @@
     )
 
 
-def factor_kernel(pivots_ref, own_ref, r1_ref, r2_ref, r3_ref, solve_ref, send_ref, all_ref):
+def factor_kernel(pivots_ref, own_ref, r1_ref, r2_ref, r3_ref, first_ref, solve_ref, send_ref, all_ref):
     row = lax.axis_index("row")
     for s, ref in enumerate((own_ref, r1_ref, r2_ref, r3_ref)):
         at = pl.multiple_of(lax.rem(row + 4 - s, 4) * BLOCK, BLOCK)
@@ -182,11 +188,14 @@
     update_t = dot(solved[WIDTH:], inverse)
     solve_ref[...] = solve_t.T
     send_ref[0:WIDTH, :] = update_t.T
-    send_ref[WIDTH:, :] = own_ref[...]
+    send_ref[WIDTH:WIDTH + BLOCK, :] = own_ref[...]
+    for c in range(2):
+        at = WIDTH + (c + 1) * BLOCK
+        send_ref[at:at + BLOCK, :] = first_ref[c]
 
 
 def finish_kernel(parents_ref, maps_ref, orders_ref, pivots_ref, top_ref, solve_ref, sent_ref,
-                  first_ref, rest_ref, lfirst_ref, lrest_ref, panel_ref, left_ref, out_ref,
+                  first_ref, rest_ref, lrest_ref, panel_ref, left_ref, out_ref,
                   hold_ref, x_ref, sem_hold, sem_x, sem_out, *, rows):
     front, row, col = lax.axis_index("front"), lax.axis_index("row"), lax.axis_index("col")
     cycles = panel_ref.shape[0]
@@ -218,9 +227,11 @@
         for s in range(child_cycles):
             places.append((pick(targets, slot_block(s, first)), c, s))
 
+    left_first = [sent_ref.at[pl.ds(WIDTH + (c + 1) * BLOCK, BLOCK)] for c in range(2)]
+
     def child_block(first, rest, c, s):
         if s == 0:
-            return first[c]
+            return first[c][...]
         return tile_block(rest, (c * (child_cycles - 1) + s - 1) * 8)
 
     lane = lax.broadcasted_iota(jnp.int32, (1, WIDTH), 1)
@@ -231,7 +242,7 @@
         pltpu.make_async_copy(panel_ref.at[at], x_ref.at[at], sem_x.at[k]).wait()
         if k == 0:
             hold_ref[0] = top_ref[...]
-            x_ref[0] = jnp.where(col == 0, top_ref[...], sent_ref[WIDTH:, :])
+            x_ref[0] = jnp.where(col == 0, top_ref[...], sent_ref[WIDTH:WIDTH + BLOCK, :])
         for place, c, s in places:
             @pl.when((place != 0) & (place // CHUNK == k))
             def _():
@@ -243,7 +254,7 @@
 
                 @pl.when(col != 0)
                 def _():
-                    x_ref[place] += child_block(lfirst_ref, lrest_ref, c, s)
+                    x_ref[place] += child_block(left_first, lrest_ref, c, s)
 
         y = dot_split(x_ref[at].reshape(CHUNK * BLOCK, WIDTH), right)
         for i in range(CHUNK):
@@ -269,30 +280,34 @@
     panel = panel[0]
     depth = 2 * (child_cycles - 1) * 8
     pieces = (BLOCK // 8, 2)
-    params = pltpu.CompilerParams(vmem_limit_bytes=32 * 2**20)
+    params = pltpu.CompilerParams(vmem_limit_bytes=24 * 2**20)
     shape = lambda *dims: jax.ShapeDtypeStruct(dims, F32)
     to_right = [(0, 1)]
 
     def exchange(value):
         return lax.all_to_all(value.reshape(fronts, -1, 128), "front", 0, 0, tiled=True)
 
+    left = lax.ppermute(panel, "col", to_right)
     spread = pl.pallas_call(
-        lambda *refs: spread_kernel(*refs, rows=rows),
-        out_shape=shape(*pieces, depth + 16, 128),
-        in_specs=[HBM, HBM], out_specs=VMEM,
+        spread_kernel, out_shape=shape(*pieces, depth + 16, 128),
+        in_specs=[HBM], out_specs=VMEM,
         scratch_shapes=[
-            pltpu.VMEM(children.shape, F32), pltpu.SMEM(row_maps.shape, jnp.int32),
-            pltpu.SemaphoreType.DMA, pltpu.SemaphoreType.DMA((2,)),
+            pltpu.VMEM(children.shape, F32), pltpu.SemaphoreType.DMA((2, child_cycles)),
         ],
         compiler_params=pltpu.CompilerParams(vmem_limit_bytes=62 * 2**20), name="spread",
-    )(row_maps, children)
+    )(children)
     spread = exchange(spread)
+    plan = pl.pallas_call(
+        lambda *refs: plan_kernel(*refs, rows=rows),
+        out_shape=jax.ShapeDtypeStruct(parents.shape, jnp.int32),
+        in_specs=[SMEM], out_specs=SMEM, name="plan",
+    )(row_maps)
     first, rest = pl.pallas_call(
-        route_kernel, out_shape=(shape(fronts, 16, 128), shape(fronts, depth, 128)),
-        in_specs=[SMEM, VMEM], out_specs=(VMEM, VMEM), compiler_params=params, name="route",
-    )(parents, spread)
+        route_kernel,
+        out_shape=(shape(fronts, 16, 128), shape(fronts, depth, 128)),
+        in_specs=[SMEM, SMEM, VMEM], out_specs=(VMEM, VMEM), compiler_params=params, name="route",
+    )(parents, plan, spread)
     first, panel = lax.optimization_barrier((first, panel))
-    left = lax.ppermute(panel, "col", to_right)
     first = exchange(first)
     panel_top = panel[0]
     top, first = pl.pallas_call(
@@ -306,16 +321,14 @@
     others = [
         lax.ppermute(top, "row", [(i, (i + s) % rows) for i in range(rows)]) for s in (1, 2, 3)
     ]
-    left_first = lax.ppermute(first, "col", to_right)
-    *others, left_first = lax.optimization_barrier((*others, left_first))
     solve, send = pl.pallas_call(
         factor_kernel,
-        out_shape=(shape(WIDTH, WIDTH), shape(WIDTH + BLOCK, WIDTH)),
-        in_specs=[SMEM, VMEM, VMEM, VMEM, VMEM], out_specs=(VMEM, VMEM),
+        out_shape=(shape(WIDTH, WIDTH), shape(WIDTH + 3 * BLOCK, WIDTH)),
+        in_specs=[SMEM] + [VMEM] * 5, out_specs=(VMEM, VMEM),
         scratch_shapes=[pltpu.VMEM((4 * BLOCK, WIDTH), F32)],
         compiler_params=params, name="factor",
         cost_estimate=pl.CostEstimate(flops=2 * 10**9, bytes_accessed=2**21, transcendentals=0),
-    )(pivots, top, *others)
+    )(pivots, top, *others, first)
     sent = lax.ppermute(send, "col", to_right)
 
     rest, solve = lax.optimization_barrier((rest, solve))
@@ -324,13 +337,13 @@
     out = pl.pallas_call(
         lambda *refs: finish_kernel(*refs, rows=rows),
         out_shape=shape(*panel.shape),
-        in_specs=[SMEM] * 4 + [VMEM] * 7 + [HBM] * 2, out_specs=HBM,
+        in_specs=[SMEM] * 4 + [VMEM] * 6 + [HBM] * 2, out_specs=HBM,
         scratch_shapes=[pltpu.VMEM(panel.shape, F32)] * 2 + [pltpu.SemaphoreType.DMA((steps,))] * 3,
-        compiler_params=pltpu.CompilerParams(vmem_limit_bytes=57 * 2**20), name="finish",
+        compiler_params=pltpu.CompilerParams(vmem_limit_bytes=24 * 2**20), name="finish",
         cost_estimate=pl.CostEstimate(flops=10**9, bytes_accessed=12 * 2**20, transcendentals=0),
     )(
         parents, row_maps, orders, pivots, top, solve, sent,
-        first, rest, left_first, left_rest, panel, left,
+        first, rest, left_rest, panel, left,
     )
     return out[None]
 

time: 110 us -> 106 us (0.964)
  blocking collectives: 38.1 us -> 0 us
  waiting for transfers between devices: 21.4 us -> 42 us
  starting transfers between devices: 19.5 us -> 30 us
  Pallas kernels: 24.7 us -> 26.4 us
  local copies, waits for them, and re-layouts: 4.06 us -> 5.22 us
    all_to_all x1 -> x0, blocking collectives: 38.1 us -> none  [exchange(): lax.all_to_all(value.reshape(fronts, -1, 128), 'front', 0, 0, tiled=True)]
    all_to_all x2 -> x3, waiting for transfers between devices: 9.49 us -> 30.9 us  [exchange(): lax.all_to_all(value.reshape(fronts, -1, 128), 'front', 0, 0, tiled=True)]
    all_to_all x2 -> x3, starting transfers between devices: 10.3 us -> 22.2 us  [exchange(): lax.all_to_all(value.reshape(fronts, -1, 128), 'front', 0, 0, tiled=True)]
    pallas_call x1 -> x2, Pallas kernels: 2.48 us -> 5.19 us  [the longest x1 2.83 us: on_device(): pl.pallas_call(lambda *refs: plan_kernel(*refs, rows=rows), out_shape=jax...]
    pallas_call x1, Pallas kernels: 9.11 us -> 7.79 us  [on_device(): pl.pallas_call(lambda *refs: finish_kernel(*refs, rows=rows), out_shape=s...]
    ppermute x1 -> x0, starting transfers between devices: 1.29 us -> none  [on_device(): left_first = lax.ppermute(first, 'col', to_right)]
    unnamed x19 -> x13, local copies, waits for them, and re-layouts: 3.14 us -> 4.31 us
  transfers between devices with their start and end apart: 9 -> 9, of which waited for: 5 -> 6; matrix products, arithmetic and copies ran while one was open for 1% -> 2% of each run, Pallas kernels for 11% -> 15%
where the time goes in v3:
time: 106 us; the launch traced here: 105 us
  waiting for transfers between devices  42 us (40%)
  starting transfers between devices  30 us (28%)
  Pallas kernels  26.4 us (25%)
  local copies, waits for them, and re-layouts  5.22 us (5%)
  between operations  1.59 us (2%)
    all_to_all x3, waiting for transfers between devices, exchange(): lax.all_to_all(value.reshape(fronts, -1, 128), 'front', 0, 0, tiled=True)  30.9 us
    all_to_all x3, starting transfers between devices, exchange(): lax.all_to_all(value.reshape(fronts, -1, 128), 'front', 0, 0, tiled=True)  22.2 us
    pallas_call x1, Pallas kernels, on_device(): pl.pallas_call(factor_kernel, out_shape=(shape(WIDTH, WIDTH), shape(WIDTH...  10.3 us
    pallas_call x1, Pallas kernels, on_device(): pl.pallas_call(lambda *refs: finish_kernel(*refs, rows=rows), out_shape=s...  7.79 us
    ppermute x1, waiting for transfers between devices, on_device(): sent = lax.ppermute(send, 'col', to_right)  5.95 us
    ppermute x3, waiting for transfers between devices, on_device(): lax.ppermute(top, 'row', [(i, (i + s) % rows) for i in range(rows)])  5.17 us
    unnamed x13, local copies, waits for them, and re-layouts  4.31 us
    ppermute x3, starting transfers between devices, on_device(): lax.ppermute(top, 'row', [(i, (i + s) % rows) for i in range(rows)])  3.85 us
  transfers between devices with their start and end apart: 9, of which 6 were waited for; matrix products, arithmetic and copies ran while one was open for 2% of the time, Pallas kernels for 15%

profile of v3, /device:TPU:1, one launch (start us, length us, event | category | flops | bytes accessed | tf_op | source)
XLA Modules:
  0.0 105.2 jit_solution(12192887659372367840)
XLA Ops:
  0.0 0.0 copy-start.5
  0.0 0.0 copy-start.3
  0.0 2.4 %spread.1 = f32[16,2,64,128]{3,2,1,0:T(8,128)} custom-call(f32[2,4,128,256]{3,2,1,0:T(8,128)} %children_ref.1), custom_call_target="tpu_custom_call" | custom-call | tf_op jit(solution)/shard_map/spread/pallas_call | solution.py:291
  2.4 11.9 %all-to-all-start = ((f32[32,64,128]{2,1,0:T(8,128)}), f32[32,64,128]{2,1,0:T(8,128)S(1)}, u32[]{:S(2)}, u32[]{:S(2)}) async-start(f32[32,64,128]{2,1,0:T(8,128)} %bitcast.13), calls=%async_computation | async-start | bytes 2097152 | tf_op jit(solution)/shard_map/all_to_all | solution.py:288
  14.3 1.3 %collective-permute-start.5 = (f32[32,128,256]{2,1,0:T(8,128)}, f32[32,128,256]{2,1,0:T(8,128)}, u32[]{:S(2)}, u32[]{:S(2)}) collective-permute-start(f32[32,128,256]{2,1,0:T(8,128)} %bitcast.7), channel_id=1, source_target_pairs={{0,1},{2,3},{4,5},{6,7},{8,9},{10,11},{12,13},{14,15},{16,17},{18,... | collective-permute-start | bytes 12582920 | tf_op jit(solution)/shard_map/ppermute | solution.py:290
  15.6 0.0 copy-done.5
  15.6 0.7 copy.9.refs_0_.refs_1_
  16.3 2.8 %plan.1.plan_ref = s32[64]{0:T(128)} custom-call(s32[64,16]{1,0:T(8,128)} %copy.9.refs_0_.refs_1_), custom_call_target="tpu_custom_call" | custom-call | tf_op jit(solution)/shard_map/plan/pallas_call | solution.py:300
  19.1 21.4 %all-to-all-done.in_ref = f32[32,64,128]{2,1,0:T(8,128)S(1)} async-done(((f32[32,64,128]{2,1,0:T(8,128)}), f32[32,64,128]{2,1,0:T(8,128)S(1)}, u32[]{:S(2)}, u32[]{:S(2)}) %all-to-all-start) | async-done | bytes 1048608 | tf_op jit(solution)/shard_map/all_to_all | solution.py:288
  40.5 0.0 copy-done.3
  40.5 0.0 copy-start.4
  40.5 0.7 copy-done.4
  41.1 1.9 %route.1 = (f32[32,16,128]{2,1,0:T(8,128)}, f32[32,48,128]{2,1,0:T(8,128)}) custom-call(s32[64]{0:T(128)S(1)} %copy-done.3, s32[64]{0:T(128)S(1)} %copy-done.4, f32[32,64,128]{2,1,0:T(8,128)S(1)} %all-to-all-done.in_ref), custom_call_target="tpu_custom_call" | custom-call | tf_op jit(solution)/shard_map/route/pallas_call | solution.py:305
  43.0 6.4 %all-to-all-start.1 = ((f32[32,16,128]{2,1,0:T(8,128)}), f32[32,16,128]{2,1,0:T(8,128)S(1)}, u32[]{:S(2)}, u32[]{:S(2)}) async-start(f32[32,16,128]{2,1,0:T(8,128)} %get-tuple-element.20), calls=%async_computation.1 | async-start | bytes 524288 | tf_op jit(solution)/shard_map/all_to_all | solution.py:288
  49.4 0.9 slice_bitcast_fusion.refs_2_
  50.3 9.5 %all-to-all-done.1 = f32[32,16,128]{2,1,0:T(8,128)S(1)} async-done(((f32[32,16,128]{2,1,0:T(8,128)}), f32[32,16,128]{2,1,0:T(8,128)S(1)}, u32[]{:S(2)}, u32[]{:S(2)}) %all-to-all-start.1) | async-done | bytes 262176 | tf_op jit(solution)/shard_map/all_to_all | solution.py:288
  59.8 0.0 copy-start.1
  59.8 0.8 copy-done.1
  60.6 1.2 %top.1 = (f32[128,256]{1,0:T(8,128)S(1)}, f32[2,128,256]{2,1,0:T(8,128)S(1)}) custom-call(s32[64]{0:T(128)S(1)} %copy-done.3, s32[64,16]{1,0:T(8,128)S(1)} %copy-done.1, f32[128,256]{1,0:T(8,128)S(1)} %slice_bitcast_fusion.refs_2_, f32[16,2,16,128]{3,2,1,0:T(8,128)S(1)} %bitcast.12), custom_call_target="tpu_custom_call" | custom-call | tf_op jit(solution)/shard_map/top/pallas_call | solution.py:313
  61.8 0.0 copy-start.2
  61.8 4.0 %all-to-all-start.2 = ((f32[32,48,128]{2,1,0:T(8,128)}), f32[32,48,128]{2,1,0:T(8,128)S(1)}, u32[]{:S(2)}, u32[]{:S(2)}) async-start(f32[32,48,128]{2,1,0:T(8,128)} %get-tuple-element.23), calls=%async_computation.2 | async-start | bytes 1572864 | tf_op jit(solution)/shard_map/all_to_all | solution.py:288
  65.8 2.8 %collective-permute-start.2 = (f32[128,256]{1,0:T(8,128)S(1)}, f32[128,256]{1,0:T(8,128)S(1)}, u32[]{:S(2)}, u32[]{:S(2)}) collective-permute-start(f32[128,256]{1,0:T(8,128)S(1)} %get-tuple-element.22.own_ref.refs_4_), channel_id=1, source_target_pairs={{0,6},{2,0},{4,2},{6,4},{1,7},{3,1},{5,3},{7,5},{8,14},{10,8},{12,... | collective-permute-start | bytes 393224 | tf_op jit(solution)/shard_map/ppermute | solution.py:322
  68.6 0.3 collective-permute-start.1
  68.9 0.7 collective-permute-start
  70.3 1.6 %collective-permute-done.2.r3_ref = f32[128,256]{1,0:T(8,128)S(1)} collective-permute-done((f32[128,256]{1,0:T(8,128)S(1)}, f32[128,256]{1,0:T(8,128)S(1)}, u32[]{:S(2)}, u32[]{:S(2)}) %collective-permute-start.2) | collective-permute-done | bytes 131104 | tf_op jit(solution)/shard_map/ppermute | solution.py:322
  71.9 2.1 %collective-permute-done.1.r2_ref = f32[128,256]{1,0:T(8,128)S(1)} collective-permute-done((f32[128,256]{1,0:T(8,128)S(1)}, f32[128,256]{1,0:T(8,128)S(1)}, u32[]{:S(2)}, u32[]{:S(2)}) %collective-permute-start.1) | collective-permute-done | bytes 131104 | tf_op jit(solution)/shard_map/ppermute | solution.py:322
  74.0 1.4 %collective-permute-done.r1_ref = f32[128,256]{1,0:T(8,128)S(1)} collective-permute-done((f32[128,256]{1,0:T(8,128)S(1)}, f32[128,256]{1,0:T(8,128)S(1)}, u32[]{:S(2)}, u32[]{:S(2)}) %collective-permute-start) | collective-permute-done | bytes 131104 | tf_op jit(solution)/shard_map/ppermute | solution.py:322
  75.4 10.3 %factor.1 = (f32[256,256]{1,0:T(8,128)S(1)}, f32[640,256]{1,0:T(8,128)S(1)}) custom-call(s32[1]{0:T(128)S(6)} %copy.11.pivots_ref.refs_3_, f32[128,256]{1,0:T(8,128)S(1)} %get-tuple-element.22.own_ref.refs_4_, f32[128,256]{1,0:T(8,128)S(1)} %collective-permute-done.r1_ref, f32[128,256]{1,0:T(8,128)S(1)} %collective-permute-done.1.r2_ref, ...), custom_call_target="tpu_custom_call" | custom-call | flops 2000000000 | bytes 2097152 | tf_op jit(solution)/shard_map/factor/pallas_call | solution.py:324
  85.8 0.0 all-to-all-done.2
  85.8 1.3 %collective-permute-start.4 = (f32[16,2,48,128]{3,2,1,0:T(8,128)S(1)}, f32[16,2,48,128]{3,2,1,0:T(8,128)S(1)}, u32[]{:S(2)}, u32[]{:S(2)}) collective-permute-start(f32[16,2,48,128]{3,2,1,0:T(8,128)S(1)} %bitcast.10), channel_id=1, source_target_pairs={{0,1},{2,3},{4,5},{6,7},{8,9},{10,11},{12,13},{14,15},{16,17},{18,... | collective-permute-start | bytes 2359304 | tf_op jit(solution)/shard_map/ppermute | solution.py:335
  87.1 1.3 %collective-permute-start.3 = (f32[640,256]{1,0:T(8,128)S(1)}, f32[640,256]{1,0:T(8,128)S(1)}, u32[]{:S(2)}, u32[]{:S(2)}) collective-permute-start(f32[640,256]{1,0:T(8,128)S(1)} %get-tuple-element.27), channel_id=1, source_target_pairs={{0,1},{2,3},{4,5},{6,7},{8,9},{10,11},{12,13},{14,15},{16,17},{18,... | collective-permute-start | bytes 1966088 | tf_op jit(solution)/shard_map/ppermute | solution.py:332
  89.1 6.0 %collective-permute-done.3.refs_6_ = f32[640,256]{1,0:T(8,128)S(1)} collective-permute-done((f32[640,256]{1,0:T(8,128)S(1)}, f32[640,256]{1,0:T(8,128)S(1)}, u32[]{:S(2)}, u32[]{:S(2)}) %collective-permute-start.3) | collective-permute-done | bytes 655392 | tf_op jit(solution)/shard_map/ppermute | solution.py:332
  95.0 0.0 collective-permute-done.5.refs_11_
  95.0 0.0 collective-permute-done.4.refs_9_
  95.0 0.0 copy-done.2
  95.0 0.0 copy-start
  95.0 2.2 %copy-done = f32[1,32,128,256]{3,2,1,0:T(8,128)S(1)} copy-done((f32[1,32,128,256]{3,2,1,0:T(8,128)S(1)}, f32[1,32,128,256]{3,2,1,0:T(8,128)}, u32[]{:S(2)}) %copy-start) | copy-done | bytes 4194328
  97.2 7.8 %finish.1 = f32[32,128,256]{2,1,0:T(8,128)} custom-call(s32[64]{0:T(128)S(1)} %copy-done.3, s32[64,16]{1,0:T(8,128)S(1)} %copy-done.2, s32[1]{0:T(128)S(6)} %copy.10.refs_2_, s32[1]{0:T(128)S(6)} %copy.11.pivots_ref.refs_3_, f32[128,256]{1,0:T(8,128)S(1)} %get-tuple-element.22.own_ref.refs_4_, f32[256,256]{1,0:T(8,128)S(1)} %get-tuple-element.26.refs_5_, ...), custom_call_target="tpu_custom_call" | custom-call | flops 1000000000 | bytes 12582912 | tf_op jit(solution)/shard_map/finish/pallas_call | solution.py:337
Async XLA Ops:
  0.0 15.6 %copy-start.5 = (s32[64,16]{0,1:T(8,128)S(1)}, s32[64,16]{0,1:T(8,128)}, u32[]{:S(2)}) copy-start(s32[64,16]{0,1:T(8,128)} %param.9) | copy-start | bytes 12292
  0.0 40.5 %copy-start.3 = (s32[64]{0:T(128)S(1)}, s32[64]{0:T(128)}, u32[]{:S(2)}) copy-start(s32[64]{0:T(128)} %refs_0_.4) | copy-start | bytes 772
  2.4 38.1 %all-to-all-start = ((f32[32,64,128]{2,1,0:T(8,128)}), f32[32,64,128]{2,1,0:T(8,128)S(1)}, u32[]{:S(2)}, u32[]{:S(2)}) async-start(f32[32,64,128]{2,1,0:T(8,128)} %bitcast.13), calls=%async_computation | async-start | bytes 2097152 | tf_op jit(solution)/shard_map/all_to_all | solution.py:288
  14.3 80.8 %collective-permute-start.5 = (f32[32,128,256]{2,1,0:T(8,128)}, f32[32,128,256]{2,1,0:T(8,128)}, u32[]{:S(2)}, u32[]{:S(2)}) collective-permute-start(f32[32,128,256]{2,1,0:T(8,128)} %bitcast.7), channel_id=1, source_target_pairs={{0,1},{2,3},{4,5},{6,7},{8,9},{10,11},{12,13},{14,15},{16,17},{18,... | collective-permute-start | bytes 12582920 | tf_op jit(solution)/shard_map/ppermute | solution.py:290
  40.5 0.7 copy-start.4
  43.0 16.8 %all-to-all-start.1 = ((f32[32,16,128]{2,1,0:T(8,128)}), f32[32,16,128]{2,1,0:T(8,128)S(1)}, u32[]{:S(2)}, u32[]{:S(2)}) async-start(f32[32,16,128]{2,1,0:T(8,128)} %get-tuple-element.20), calls=%async_computation.1 | async-start | bytes 524288 | tf_op jit(solution)/shard_map/all_to_all | solution.py:288
  59.8 0.8 copy-start.1
  61.8 33.3 %copy-start.2 = (s32[64,16]{1,0:T(8,128)S(1)}, s32[64,16]{1,0:T(8,128)}, u32[]{:S(2)}) copy-start(s32[64,16]{1,0:T(8,128)} %copy.9.refs_0_.refs_1_) | copy-start | bytes 12292
  61.8 24.0 %all-to-all-start.2 = ((f32[32,48,128]{2,1,0:T(8,128)}), f32[32,48,128]{2,1,0:T(8,128)S(1)}, u32[]{:S(2)}, u32[]{:S(2)}) async-start(f32[32,48,128]{2,1,0:T(8,128)} %get-tuple-element.23), calls=%async_computation.2 | async-start | bytes 1572864 | tf_op jit(solution)/shard_map/all_to_all | solution.py:288
  65.8 6.1 %collective-permute-start.2 = (f32[128,256]{1,0:T(8,128)S(1)}, f32[128,256]{1,0:T(8,128)S(1)}, u32[]{:S(2)}, u32[]{:S(2)}) collective-permute-start(f32[128,256]{1,0:T(8,128)S(1)} %get-tuple-element.22.own_ref.refs_4_), channel_id=1, source_target_pairs={{0,6},{2,0},{4,2},{6,4},{1,7},{3,1},{5,3},{7,5},{8,14},{10,8},{12,... | collective-permute-start | bytes 393224 | tf_op jit(solution)/shard_map/ppermute | solution.py:322
  68.6 5.4 %collective-permute-start.1 = (f32[128,256]{1,0:T(8,128)S(1)}, f32[128,256]{1,0:T(8,128)S(1)}, u32[]{:S(2)}, u32[]{:S(2)}) collective-permute-start(f32[128,256]{1,0:T(8,128)S(1)} %get-tuple-element.22.own_ref.refs_4_), channel_id=1, source_target_pairs={{0,4},{2,6},{4,0},{6,2},{1,5},{3,7},{5,1},{7,3},{8,12},{10,14},{12... | collective-permute-start | bytes 393224 | tf_op jit(solution)/shard_map/ppermute | solution.py:322
  68.9 6.5 %collective-permute-start = (f32[128,256]{1,0:T(8,128)S(1)}, f32[128,256]{1,0:T(8,128)S(1)}, u32[]{:S(2)}, u32[]{:S(2)}) collective-permute-start(f32[128,256]{1,0:T(8,128)S(1)} %get-tuple-element.22.own_ref.refs_4_), channel_id=1, source_target_pairs={{0,2},{2,4},{4,6},{6,0},{1,3},{3,5},{5,7},{7,1},{8,10},{10,12},{12... | collective-permute-start | bytes 393224 | tf_op jit(solution)/shard_map/ppermute | solution.py:322
  85.8 9.2 %collective-permute-start.4 = (f32[16,2,48,128]{3,2,1,0:T(8,128)S(1)}, f32[16,2,48,128]{3,2,1,0:T(8,128)S(1)}, u32[]{:S(2)}, u32[]{:S(2)}) collective-permute-start(f32[16,2,48,128]{3,2,1,0:T(8,128)S(1)} %bitcast.10), channel_id=1, source_target_pairs={{0,1},{2,3},{4,5},{6,7},{8,9},{10,11},{12,13},{14,15},{16,17},{18,... | collective-permute-start | bytes 2359304 | tf_op jit(solution)/shard_map/ppermute | solution.py:335
  87.1 7.9 %collective-permute-start.3 = (f32[640,256]{1,0:T(8,128)S(1)}, f32[640,256]{1,0:T(8,128)S(1)}, u32[]{:S(2)}, u32[]{:S(2)}) collective-permute-start(f32[640,256]{1,0:T(8,128)S(1)} %get-tuple-element.27), channel_id=1, source_target_pairs={{0,1},{2,3},{4,5},{6,7},{8,9},{10,11},{12,13},{14,15},{16,17},{18,... | collective-permute-start | bytes 1966088 | tf_op jit(solution)/shard_map/ppermute | solution.py:332
  95.0 2.2 %copy-start = (f32[1,32,128,256]{3,2,1,0:T(8,128)S(1)}, f32[1,32,128,256]{3,2,1,0:T(8,128)}, u32[]{:S(2)}) copy-start(f32[1,32,128,256]{3,2,1,0:T(8,128)} %param.6) | copy-start | bytes 12582916

commit v4 on v3

--- a/solution.py
+++ b/solution.py
@@ -68,7 +68,7 @@
     return found
 
 
-def spread_kernel(children_ref, out_ref, hold_ref, sem):
+def spread_kernel(children_ref, panel_ref, out_ref, top_ref, hold_ref, sem, sem_top):
     cycles = children_ref.shape[1]
     blocks = [(c, i) for c in range(2) for i in range(cycles)]
     copies = [
@@ -77,11 +77,14 @@
     ]
     for copy in copies:
         copy.start()
+    top = pltpu.make_async_copy(panel_ref.at[0], top_ref, sem_top)
+    top.start()
     for n, (c, i) in enumerate(blocks):
         copies[n].wait()
         for half in range(2):
             tiles = hold_ref[c, i, :, half * 128:(half + 1) * 128]
             out_ref[:, half, n * 8:(n + 1) * 8, :] = tiles.reshape(BLOCK // 8, 8, 128)
+    top.wait()
 
 
 def plan_kernel(maps_ref, out_ref, *, rows):
@@ -288,14 +291,15 @@
         return lax.all_to_all(value.reshape(fronts, -1, 128), "front", 0, 0, tiled=True)
 
     left = lax.ppermute(panel, "col", to_right)
-    spread = pl.pallas_call(
-        spread_kernel, out_shape=shape(*pieces, depth + 16, 128),
-        in_specs=[HBM], out_specs=VMEM,
+    spread, panel_top = pl.pallas_call(
+        spread_kernel, out_shape=(shape(*pieces, depth + 16, 128), shape(BLOCK, WIDTH)),
+        in_specs=[HBM, HBM], out_specs=(VMEM, VMEM),
         scratch_shapes=[
             pltpu.VMEM(children.shape, F32), pltpu.SemaphoreType.DMA((2, child_cycles)),
+            pltpu.SemaphoreType.DMA,
         ],
         compiler_params=pltpu.CompilerParams(vmem_limit_bytes=62 * 2**20), name="spread",
-    )(children)
+    )(children, panel)
     spread = exchange(spread)
     plan = pl.pallas_call(
         lambda *refs: plan_kernel(*refs, rows=rows),
@@ -307,9 +311,7 @@
         out_shape=(shape(fronts, 16, 128), shape(fronts, depth, 128)),
         in_specs=[SMEM, SMEM, VMEM], out_specs=(VMEM, VMEM), compiler_params=params, name="route",
     )(parents, plan, spread)
-    first, panel = lax.optimization_barrier((first, panel))
     first = exchange(first)
-    panel_top = panel[0]
     top, first = pl.pallas_call(
         lambda *refs: top_kernel(*refs, rows=rows),
         out_shape=(shape(BLOCK, WIDTH), shape(2, BLOCK, WIDTH)),

time: 106 us -> 106 us (level)
  blocking collectives: 0 us -> 16.5 us
  waiting for transfers between devices: 42 us -> 32.5 us
  starting transfers between devices: 30 us -> 23.6 us
    all_to_all x0 -> x1, blocking collectives: none -> 16.5 us  [exchange(): lax.all_to_all(value.reshape(fronts, -1, 128), 'front', 0, 0, tiled=True)]
    all_to_all x3 -> x2, waiting for transfers between devices: 30.9 us -> 21.4 us  [exchange(): lax.all_to_all(value.reshape(fronts, -1, 128), 'front', 0, 0, tiled=True)]
    all_to_all x3 -> x2, starting transfers between devices: 22.2 us -> 15.9 us  [exchange(): lax.all_to_all(value.reshape(fronts, -1, 128), 'front', 0, 0, tiled=True)]
    unnamed x13 -> x15, local copies, waits for them, and re-layouts: 4.31 us -> 5.15 us
  transfers between devices with their start and end apart: 9 -> 8, of which waited for: 6 -> 5; matrix products, arithmetic and copies ran while one was open for 2% -> 1% of each run, Pallas kernels for 15% -> 15%
where the time goes in v4:
time: 106 us
  waiting for transfers between devices  32.5 us (31%)
  Pallas kernels  26.4 us (25%)
  starting transfers between devices  23.6 us (22%)
  blocking collectives  16.5 us (16%)
  local copies, waits for them, and re-layouts  5.15 us (5%)
  between operations  1.58 us (1%)
    all_to_all x2, waiting for transfers between devices, exchange(): lax.all_to_all(value.reshape(fronts, -1, 128), 'front', 0, 0, tiled=True)  21.4 us
    all_to_all x1, blocking collectives, exchange(): lax.all_to_all(value.reshape(fronts, -1, 128), 'front', 0, 0, tiled=True)  16.5 us
    all_to_all x2, starting transfers between devices, exchange(): lax.all_to_all(value.reshape(fronts, -1, 128), 'front', 0, 0, tiled=True)  15.9 us
    pallas_call x1, Pallas kernels, on_device(): pl.pallas_call(factor_kernel, out_shape=(shape(WIDTH, WIDTH), shape(WIDTH...  10.3 us
    pallas_call x1, Pallas kernels, on_device(): pl.pallas_call(lambda *refs: finish_kernel(*refs, rows=rows), out_shape=s...  7.79 us
    ppermute x1, waiting for transfers between devices, on_device(): sent = lax.ppermute(send, 'col', to_right)  5.95 us
    ppermute x3, waiting for transfers between devices, on_device(): lax.ppermute(top, 'row', [(i, (i + s) % rows) for i in range(rows)])  5.17 us
    unnamed x15, local copies, waits for them, and re-layouts  5.15 us
  transfers between devices with their start and end apart: 8, of which 5 were waited for; matrix products, arithmetic and copies ran while one was open for 1% of the time, Pallas kernels for 15%

profile of v4, /device:TPU:1, one launch (start us, length us, event | category | flops | bytes accessed | tf_op | source)
XLA Modules:
  0.0 105.8 jit_solution(5293986062845842379)
XLA Ops:
  0.0 0.0 copy-start.6
  0.0 0.0 copy-start.4
  0.0 2.4 %spread.1 = (f32[16,2,64,128]{3,2,1,0:T(8,128)}, f32[128,256]{1,0:T(8,128)}) custom-call(f32[2,4,128,256]{3,2,1,0:T(8,128)} %children_ref.1, f32[32,128,256]{2,1,0:T(8,128)} %bitcast.5), custom_call_target="tpu_custom_call" | custom-call | tf_op jit(solution)/shard_map/spread/pallas_call | solution.py:294
  2.4 11.9 %all-to-all-start = ((f32[32,64,128]{2,1,0:T(8,128)}), f32[32,64,128]{2,1,0:T(8,128)S(1)}, u32[]{:S(2)}, u32[]{:S(2)}) async-start(f32[32,64,128]{2,1,0:T(8,128)} %bitcast.11), calls=%async_computation | async-start | bytes 2097152 | tf_op jit(solution)/shard_map/all_to_all | solution.py:291
  14.3 1.3 %collective-permute-start.5 = (f32[32,128,256]{2,1,0:T(8,128)}, f32[32,128,256]{2,1,0:T(8,128)}, u32[]{:S(2)}, u32[]{:S(2)}) collective-permute-start(f32[32,128,256]{2,1,0:T(8,128)} %bitcast.6), channel_id=1, source_target_pairs={{0,1},{2,3},{4,5},{6,7},{8,9},{10,11},{12,13},{14,15},{16,17},{18,... | collective-permute-start | bytes 12582920 | tf_op jit(solution)/shard_map/ppermute | solution.py:293
  15.6 0.0 copy-done.6
  15.6 0.7 copy.9.refs_0_.refs_1_
  16.3 2.8 %plan.1.plan_ref = s32[64]{0:T(128)} custom-call(s32[64,16]{1,0:T(8,128)} %copy.9.refs_0_.refs_1_), custom_call_target="tpu_custom_call" | custom-call | tf_op jit(solution)/shard_map/plan/pallas_call | solution.py:304
  19.2 21.4 %all-to-all-done.in_ref = f32[32,64,128]{2,1,0:T(8,128)S(1)} async-done(((f32[32,64,128]{2,1,0:T(8,128)}), f32[32,64,128]{2,1,0:T(8,128)S(1)}, u32[]{:S(2)}, u32[]{:S(2)}) %all-to-all-start) | async-done | bytes 1048608 | tf_op jit(solution)/shard_map/all_to_all | solution.py:291
  40.5 0.0 copy-done.4
  40.5 0.0 copy-start.5
  40.5 0.6 copy-done.5
  41.1 1.8 %route.1 = (f32[32,16,128]{2,1,0:T(8,128)S(1)}, f32[32,48,128]{2,1,0:T(8,128)}) custom-call(s32[64]{0:T(128)S(1)} %copy-done.4, s32[64]{0:T(128)S(1)} %copy-done.5, f32[32,64,128]{2,1,0:T(8,128)S(1)} %all-to-all-done.in_ref), custom_call_target="tpu_custom_call" | custom-call | tf_op jit(solution)/shard_map/route/pallas_call | solution.py:309
  42.9 16.5 %all_to_all.15 = f32[32,16,128]{2,1,0:T(8,128)S(1)} all-to-all(f32[32,16,128]{2,1,0:T(8,128)S(1)} %get-tuple-element.20), channel_id=1, replica_groups=mesh['front'=32,'row'=4,'col'=2] {'front'}, dimensions={0} | all-to-all | bytes 524288 | tf_op jit(solution)/shard_map/all_to_all | solution.py:291
  59.5 0.0 copy-start.1
  59.5 0.8 copy-done.1
  60.2 0.0 copy-start.3
  60.2 0.9 copy-done.3
  61.1 1.2 %top.1 = (f32[128,256]{1,0:T(8,128)S(1)}, f32[2,128,256]{2,1,0:T(8,128)S(1)}) custom-call(s32[64]{0:T(128)S(1)} %copy-done.4, s32[64,16]{1,0:T(8,128)S(1)} %copy-done.1, f32[128,256]{1,0:T(8,128)S(1)} %copy-done.3, f32[16,2,16,128]{3,2,1,0:T(8,128)S(1)} %bitcast.10), custom_call_target="tpu_custom_call" | custom-call | tf_op jit(solution)/shard_map/top/pallas_call | solution.py:315
  62.3 0.0 copy-start.2
  62.4 4.0 %all-to-all-start.2 = ((f32[32,48,128]{2,1,0:T(8,128)}), f32[32,48,128]{2,1,0:T(8,128)S(1)}, u32[]{:S(2)}, u32[]{:S(2)}) async-start(f32[32,48,128]{2,1,0:T(8,128)} %get-tuple-element.23), calls=%async_computation.2 | async-start | bytes 1572864 | tf_op jit(solution)/shard_map/all_to_all | solution.py:291
  66.4 2.8 %collective-permute-start.2 = (f32[128,256]{1,0:T(8,128)S(1)}, f32[128,256]{1,0:T(8,128)S(1)}, u32[]{:S(2)}, u32[]{:S(2)}) collective-permute-start(f32[128,256]{1,0:T(8,128)S(1)} %get-tuple-element.22.own_ref.refs_4_), channel_id=1, source_target_pairs={{0,6},{2,0},{4,2},{6,4},{1,7},{3,1},{5,3},{7,5},{8,14},{10,8},{12,... | collective-permute-start | bytes 393224 | tf_op jit(solution)/shard_map/ppermute | solution.py:324
  69.2 0.3 collective-permute-start.1
  69.5 0.7 collective-permute-start
  70.9 1.6 %collective-permute-done.2.r3_ref = f32[128,256]{1,0:T(8,128)S(1)} collective-permute-done((f32[128,256]{1,0:T(8,128)S(1)}, f32[128,256]{1,0:T(8,128)S(1)}, u32[]{:S(2)}, u32[]{:S(2)}) %collective-permute-start.2) | collective-permute-done | bytes 131104 | tf_op jit(solution)/shard_map/ppermute | solution.py:324
  72.5 2.1 %collective-permute-done.1.r2_ref = f32[128,256]{1,0:T(8,128)S(1)} collective-permute-done((f32[128,256]{1,0:T(8,128)S(1)}, f32[128,256]{1,0:T(8,128)S(1)}, u32[]{:S(2)}, u32[]{:S(2)}) %collective-permute-start.1) | collective-permute-done | bytes 131104 | tf_op jit(solution)/shard_map/ppermute | solution.py:324
  74.6 1.4 %collective-permute-done.r1_ref = f32[128,256]{1,0:T(8,128)S(1)} collective-permute-done((f32[128,256]{1,0:T(8,128)S(1)}, f32[128,256]{1,0:T(8,128)S(1)}, u32[]{:S(2)}, u32[]{:S(2)}) %collective-permute-start) | collective-permute-done | bytes 131104 | tf_op jit(solution)/shard_map/ppermute | solution.py:324
  76.0 10.3 %factor.1 = (f32[256,256]{1,0:T(8,128)S(1)}, f32[640,256]{1,0:T(8,128)S(1)}) custom-call(s32[1]{0:T(128)S(6)} %copy.11.pivots_ref.refs_3_, f32[128,256]{1,0:T(8,128)S(1)} %get-tuple-element.22.own_ref.refs_4_, f32[128,256]{1,0:T(8,128)S(1)} %collective-permute-done.r1_ref, f32[128,256]{1,0:T(8,128)S(1)} %collective-permute-done.1.r2_ref, ...), custom_call_target="tpu_custom_call" | custom-call | flops 2000000000 | bytes 2097152 | tf_op jit(solution)/shard_map/factor/pallas_call | solution.py:326
  86.4 0.0 all-to-all-done.2
  86.4 1.3 %collective-permute-start.4 = (f32[16,2,48,128]{3,2,1,0:T(8,128)S(1)}, f32[16,2,48,128]{3,2,1,0:T(8,128)S(1)}, u32[]{:S(2)}, u32[]{:S(2)}) collective-permute-start(f32[16,2,48,128]{3,2,1,0:T(8,128)S(1)} %bitcast.8), channel_id=1, source_target_pairs={{0,1},{2,3},{4,5},{6,7},{8,9},{10,11},{12,13},{14,15},{16,17},{18,... | collective-permute-start | bytes 2359304 | tf_op jit(solution)/shard_map/ppermute | solution.py:337
  87.7 1.3 %collective-permute-start.3 = (f32[640,256]{1,0:T(8,128)S(1)}, f32[640,256]{1,0:T(8,128)S(1)}, u32[]{:S(2)}, u32[]{:S(2)}) collective-permute-start(f32[640,256]{1,0:T(8,128)S(1)} %get-tuple-element.27), channel_id=1, source_target_pairs={{0,1},{2,3},{4,5},{6,7},{8,9},{10,11},{12,13},{14,15},{16,17},{18,... | collective-permute-start | bytes 1966088 | tf_op jit(solution)/shard_map/ppermute | solution.py:334
  89.6 6.0 %collective-permute-done.3.refs_6_ = f32[640,256]{1,0:T(8,128)S(1)} collective-permute-done((f32[640,256]{1,0:T(8,128)S(1)}, f32[640,256]{1,0:T(8,128)S(1)}, u32[]{:S(2)}, u32[]{:S(2)}) %collective-permute-start.3) | collective-permute-done | bytes 655392 | tf_op jit(solution)/shard_map/ppermute | solution.py:334
  95.6 0.0 collective-permute-done.5.refs_11_
  95.6 0.0 collective-permute-done.4.refs_9_
  95.6 0.0 copy-done.2
  95.6 0.0 copy-start
  95.6 2.2 %copy-done = f32[1,32,128,256]{3,2,1,0:T(8,128)S(1)} copy-done((f32[1,32,128,256]{3,2,1,0:T(8,128)S(1)}, f32[1,32,128,256]{3,2,1,0:T(8,128)}, u32[]{:S(2)}) %copy-start) | copy-done | bytes 4194328
  97.8 7.8 %finish.1 = f32[32,128,256]{2,1,0:T(8,128)} custom-call(s32[64]{0:T(128)S(1)} %copy-done.4, s32[64,16]{1,0:T(8,128)S(1)} %copy-done.2, s32[1]{0:T(128)S(6)} %copy.10.refs_2_, s32[1]{0:T(128)S(6)} %copy.11.pivots_ref.refs_3_, f32[128,256]{1,0:T(8,128)S(1)} %get-tuple-element.22.own_ref.refs_4_, f32[256,256]{1,0:T(8,128)S(1)} %get-tuple-element.26.refs_5_, ...), custom_call_target="tpu_custom_call" | custom-call | flops 1000000000 | bytes 12582912 | tf_op jit(solution)/shard_map/finish/pallas_call | solution.py:339
Async XLA Ops:
  0.0 15.6 %copy-start.6 = (s32[64,16]{0,1:T(8,128)S(1)}, s32[64,16]{0,1:T(8,128)}, u32[]{:S(2)}) copy-start(s32[64,16]{0,1:T(8,128)} %param.9) | copy-start | bytes 12292
  0.0 40.5 %copy-start.4 = (s32[64]{0:T(128)S(1)}, s32[64]{0:T(128)}, u32[]{:S(2)}) copy-start(s32[64]{0:T(128)} %refs_0_.4) | copy-start | bytes 772
  2.4 38.1 %all-to-all-start = ((f32[32,64,128]{2,1,0:T(8,128)}), f32[32,64,128]{2,1,0:T(8,128)S(1)}, u32[]{:S(2)}, u32[]{:S(2)}) async-start(f32[32,64,128]{2,1,0:T(8,128)} %bitcast.11), calls=%async_computation | async-start | bytes 2097152 | tf_op jit(solution)/shard_map/all_to_all | solution.py:291
  14.3 81.3 %collective-permute-start.5 = (f32[32,128,256]{2,1,0:T(8,128)}, f32[32,128,256]{2,1,0:T(8,128)}, u32[]{:S(2)}, u32[]{:S(2)}) collective-permute-start(f32[32,128,256]{2,1,0:T(8,128)} %bitcast.6), channel_id=1, source_target_pairs={{0,1},{2,3},{4,5},{6,7},{8,9},{10,11},{12,13},{14,15},{16,17},{18,... | collective-permute-start | bytes 12582920 | tf_op jit(solution)/shard_map/ppermute | solution.py:293
  40.5 0.6 copy-start.5
  59.5 0.8 copy-start.1
  60.2 0.9 copy-start.3
  62.3 33.3 %copy-start.2 = (s32[64,16]{1,0:T(8,128)S(1)}, s32[64,16]{1,0:T(8,128)}, u32[]{:S(2)}) copy-start(s32[64,16]{1,0:T(8,128)} %copy.9.refs_0_.refs_1_) | copy-start | bytes 12292
  62.4 24.0 %all-to-all-start.2 = ((f32[32,48,128]{2,1,0:T(8,128)}), f32[32,48,128]{2,1,0:T(8,128)S(1)}, u32[]{:S(2)}, u32[]{:S(2)}) async-start(f32[32,48,128]{2,1,0:T(8,128)} %get-tuple-element.23), calls=%async_computation.2 | async-start | bytes 1572864 | tf_op jit(solution)/shard_map/all_to_all | solution.py:291
  66.4 6.1 %collective-permute-start.2 = (f32[128,256]{1,0:T(8,128)S(1)}, f32[128,256]{1,0:T(8,128)S(1)}, u32[]{:S(2)}, u32[]{:S(2)}) collective-permute-start(f32[128,256]{1,0:T(8,128)S(1)} %get-tuple-element.22.own_ref.refs_4_), channel_id=1, source_target_pairs={{0,6},{2,0},{4,2},{6,4},{1,7},{3,1},{5,3},{7,5},{8,14},{10,8},{12,... | collective-permute-start | bytes 393224 | tf_op jit(solution)/shard_map/ppermute | solution.py:324
  69.2 5.4 %collective-permute-start.1 = (f32[128,256]{1,0:T(8,128)S(1)}, f32[128,256]{1,0:T(8,128)S(1)}, u32[]{:S(2)}, u32[]{:S(2)}) collective-permute-start(f32[128,256]{1,0:T(8,128)S(1)} %get-tuple-element.22.own_ref.refs_4_), channel_id=1, source_target_pairs={{0,4},{2,6},{4,0},{6,2},{1,5},{3,7},{5,1},{7,3},{8,12},{10,14},{12... | collective-permute-start | bytes 393224 | tf_op jit(solution)/shard_map/ppermute | solution.py:324
  69.5 6.5 %collective-permute-start = (f32[128,256]{1,0:T(8,128)S(1)}, f32[128,256]{1,0:T(8,128)S(1)}, u32[]{:S(2)}, u32[]{:S(2)}) collective-permute-start(f32[128,256]{1,0:T(8,128)S(1)} %get-tuple-element.22.own_ref.refs_4_), channel_id=1, source_target_pairs={{0,2},{2,4},{4,6},{6,0},{1,3},{3,5},{5,7},{7,1},{8,10},{10,12},{12... | collective-permute-start | bytes 393224 | tf_op jit(solution)/shard_map/ppermute | solution.py:324
  86.4 9.2 %collective-permute-start.4 = (f32[16,2,48,128]{3,2,1,0:T(8,128)S(1)}, f32[16,2,48,128]{3,2,1,0:T(8,128)S(1)}, u32[]{:S(2)}, u32[]{:S(2)}) collective-permute-start(f32[16,2,48,128]{3,2,1,0:T(8,128)S(1)} %bitcast.8), channel_id=1, source_target_pairs={{0,1},{2,3},{4,5},{6,7},{8,9},{10,11},{12,13},{14,15},{16,17},{18,... | collective-permute-start | bytes 2359304 | tf_op jit(solution)/shard_map/ppermute | solution.py:337
  87.7 7.9 %collective-permute-start.3 = (f32[640,256]{1,0:T(8,128)S(1)}, f32[640,256]{1,0:T(8,128)S(1)}, u32[]{:S(2)}, u32[]{:S(2)}) collective-permute-start(f32[640,256]{1,0:T(8,128)S(1)} %get-tuple-element.27), channel_id=1, source_target_pairs={{0,1},{2,3},{4,5},{6,7},{8,9},{10,11},{12,13},{14,15},{16,17},{18,... | collective-permute-start | bytes 1966088 | tf_op jit(solution)/shard_map/ppermute | solution.py:334
  95.6 2.2 %copy-start = (f32[1,32,128,256]{3,2,1,0:T(8,128)S(1)}, f32[1,32,128,256]{3,2,1,0:T(8,128)}, u32[]{:S(2)}) copy-start(f32[1,32,128,256]{3,2,1,0:T(8,128)} %param.6) | copy-start | bytes 12582916
